TPU v7x, 512 devices: a whole 4x4x16 slice. The times are simulated.
512 devices in a mesh: pipe: 8 (over z_hi, core), expert: 64 (over z_lo, y, x).
Axes of the slice: x: 4, y: 4, z: 16 (z_hi: 4, z_lo: 4; z = z_hi * 4 + z_lo), core: 2. Of those that a mesh axis runs over, the one named last changes fastest.
Arguments:
- held_acts: bfloat16 [8, 1024, 3584], P('pipe', 'expert'), may hold values from -6 to 6
- held_grads: bfloat16 [8, 1024, 3584], P('pipe', 'expert'), may hold values from -6 to 6
- saved_inputs: bfloat16 [8, 1024, 3584], P('pipe', 'expert'), may hold values from -6 to 6
- norm_gain: float32 [8, 3584], P('pipe'), may hold values from 0.25 to 1.75
- gate_proj: bfloat16 [8, 3584, 8192], P('pipe', None, 'expert'), may hold values from -0.09375 to 0.09375
- up_proj: bfloat16 [8, 3584, 8192], P('pipe', None, 'expert'), may hold values from -0.09375 to 0.09375
- down_proj: bfloat16 [8, 8192, 3584], P('pipe', 'expert'), may hold values from -0.1875 to 0.1875
- fwd_routes: int32 [8, 1024, 2], P('pipe', 'expert'), may hold values from 0 to 7, all different within a row; in each aligned block of 16 rows (0 to 15, 16 to 31, ..., all dimensions but the last counted through in order) at most 6 rows name the same one
- fwd_gates: float32 [8, 1024, 2], P('pipe', 'expert'), may hold values from 0.1 to 1
- bwd_routes: int32 [8, 1024, 2], P('pipe', 'expert'), may hold values from 0 to 7, all different within a row; in each aligned block of 16 rows (0 to 15, 16 to 31, ..., all dimensions but the last counted through in order) at most 6 rows name the same one
- bwd_gates: float32 [8, 1024, 2], P('pipe', 'expert'), may hold values from 0.1 to 1
Outputs:
- section_outputs: bfloat16 [8, 1024, 3584], P('pipe', 'expert')
- input_grads: bfloat16 [8, 1024, 3584], P('pipe', 'expert')
Inputs may be any that keep to these rules, and one draw needn't show every extreme that they name: `fwd_routes`: within the rows of one device (aligned blocks of 16 rows) no expert is named by more than 6 tokens, a bound that some block reaches; a token's experts differ. `bwd_routes`: as for fwd_routes.
All inputs are finite; a program needn't handle non-finite values.
Results may differ from a plain program's by a relative error of at most 0.0095.
Values may be sent and summed in bfloat16 or wider, within the bound.
A program may use at most 128 MiB of HBM per device.

v0:
```python
import jax
import jax.numpy as jnp
from jax import lax
from jax.sharding import PartitionSpec as P

SLICE = 8


NORM_EPSILON = 1e-06


def shifted(block, axis, distance):
    devices = range(lax.axis_size(axis))
    route = [((i - distance) % len(devices), i) for i in devices]
    return lax.ppermute(block, axis, route)


def slot_tables(routes, gates, experts, most):
    token_count, picks = routes.shape
    chosen = (routes[:, :, None] == jnp.arange(experts, dtype=jnp.int32)[None, None, :]).astype(
        jnp.float32
    )
    chosen = chosen.reshape(token_count * picks, experts)
    earlier = jnp.cumsum(chosen, axis=0) - chosen
    places = jnp.arange(most, dtype=jnp.int32).astype(jnp.float32)
    placed = chosen[:, :, None] * (earlier[:, :, None] == places[None, None, :]).astype(jnp.float32)
    placed = placed.reshape(token_count, picks, experts * most)
    expert_selection = jnp.sum(placed, axis=1)
    routing_weights = jnp.sum(placed * gates[:, :, None], axis=1)
    return (expert_selection, routing_weights)


def normalize(inputs, gain):
    routing_values = inputs.astype(jnp.float32)
    scale = lax.rsqrt(
        jnp.mean(routing_values * routing_values, axis=-1, keepdims=True) + NORM_EPSILON
    )
    return ((routing_values * scale * gain[None, :]).astype(jnp.bfloat16), scale)


def dispatched_rows(expert_selection, routing_values, experts, most):
    width = routing_values.shape[1]
    expert_slots = jnp.einsum(
        "tk,td->kd",
        expert_selection.astype(jnp.bfloat16),
        routing_values,
        preferred_element_type=jnp.float32,
    ).astype(jnp.bfloat16)
    expert_slots = expert_slots.reshape(experts, 1, most, width)
    expert_slots = jnp.broadcast_to(expert_slots, (experts, SLICE, most, width))
    return expert_slots.reshape(experts * SLICE, most, width)


def local(
    held_acts,
    held_grads,
    saved_inputs,
    norm_gain,
    gate_proj,
    up_proj,
    down_proj,
    fwd_routes,
    fwd_gates,
    bwd_routes,
    bwd_gates,
):
    section_in = shifted(held_acts, "pipe", 1)[0]
    incoming = shifted(held_grads, "pipe", -1)[0]
    gain = norm_gain[0]
    w_gate = gate_proj[0]
    w_up = up_proj[0]
    w_down = down_proj[0]
    devices = lax.axis_size("expert")
    experts = devices // SLICE
    token_count = held_acts.shape[1]
    width = held_acts.shape[2]
    picks = fwd_routes.shape[2]
    most = min(token_count, 3 * token_count * picks // (2 * experts))
    normed_input, unused_scale = normalize(section_in, gain)
    expert_selection, routing_weights = slot_tables(fwd_routes[0], fwd_gates[0], experts, most)
    normed_back, scale = normalize(saved_inputs[0], gain)
    select_back, weighs_back = slot_tables(bwd_routes[0], bwd_gates[0], experts, most)
    sent_rows = dispatched_rows(expert_selection, normed_input, experts, most)
    sent_back = dispatched_rows(select_back, normed_back, experts, most)
    sent_cot = dispatched_rows(select_back, incoming, experts, most)
    rows = lax.all_to_all(sent_rows, "expert", split_axis=0, concat_axis=0, tiled=True)
    back_rows = lax.all_to_all(sent_back, "expert", split_axis=0, concat_axis=0, tiled=True)
    back_cot = lax.all_to_all(sent_cot, "expert", split_axis=0, concat_axis=0, tiled=True)
    shape = rows.shape
    flat = rows.reshape(-1, width)
    gate = jnp.dot(flat, w_gate, preferred_element_type=jnp.float32)
    upper = jnp.dot(flat, w_up, preferred_element_type=jnp.float32)
    active_hidden = (jax.nn.silu(gate) * upper).astype(jnp.bfloat16)
    forward_part = jnp.dot(active_hidden, w_down, preferred_element_type=jnp.float32).astype(
        jnp.bfloat16
    )
    flat_back = back_rows.reshape(-1, width)
    gate_back = jnp.dot(flat_back, w_gate, preferred_element_type=jnp.float32)
    upper_back = jnp.dot(flat_back, w_up, preferred_element_type=jnp.float32)
    sigma = jax.nn.sigmoid(gate_back)
    d_active = jnp.dot(back_cot.reshape(-1, width), w_down.T, preferred_element_type=jnp.float32)
    d_gate = (d_active * upper_back * sigma * (1.0 + gate_back * (1.0 - sigma))).astype(
        jnp.bfloat16
    )
    d_upper = (d_active * gate_back * sigma).astype(jnp.bfloat16)
    grad_part = jnp.dot(d_gate, w_gate.T, preferred_element_type=jnp.float32)
    grad_part = grad_part + jnp.dot(d_upper, w_up.T, preferred_element_type=jnp.float32)
    forward_part, grad_part = (
        forward_part.reshape(shape),
        grad_part.astype(jnp.bfloat16).reshape(shape),
    )
    forward_back, grad_back = (
        lax.all_to_all(forward_part, "expert", split_axis=0, concat_axis=0, tiled=True),
        lax.all_to_all(grad_part, "expert", split_axis=0, concat_axis=0, tiled=True),
    )
    forward_sum = jnp.sum(
        forward_back.reshape(experts, SLICE, most, width).astype(jnp.float32), axis=1
    )
    forward_sum = forward_sum.reshape(experts * most, width)
    grad_sum = jnp.sum(grad_back.reshape(experts, SLICE, most, width).astype(jnp.float32), axis=1)
    grad_sum = grad_sum.reshape(experts * most, width)
    branch = jnp.dot(routing_weights, forward_sum, precision=lax.Precision.HIGHEST)
    outputs = (section_in.astype(jnp.float32) + branch).astype(jnp.bfloat16)
    d_normed = jnp.dot(weighs_back, grad_sum, precision=lax.Precision.HIGHEST)
    routing_values = saved_inputs[0].astype(jnp.float32)
    scaled = d_normed * gain[None, :]
    d_input = scale * scaled - routing_values * scale * scale * scale * jnp.mean(
        scaled * routing_values, axis=-1, keepdims=True
    )
    input_grads = (incoming.astype(jnp.float32) + d_input).astype(jnp.bfloat16)
    return (outputs[None], input_grads[None])


def solution(mesh):
    return jax.shard_map(
        local,
        mesh=mesh,
        in_specs=(
            P("pipe", "expert", None),
            P("pipe", "expert", None),
            P("pipe", "expert", None),
            P("pipe", None),
            P("pipe", None, "expert"),
            P("pipe", None, "expert"),
            P("pipe", "expert", None),
            P("pipe", "expert", None),
            P("pipe", "expert", None),
            P("pipe", "expert", None),
            P("pipe", "expert", None),
        ),
        out_specs=(P("pipe", "expert", None), P("pipe", "expert", None)),
        check_vma=False,
    )
```

profile of v0, /device:TPU:128, one launch (start us, length us, event | category | flops | bytes accessed | tf_op | source)
XLA Modules:
  0.0 490.7 jit_solution(7517445190213111766)
XLA Ops:
  0.7 0.8 copy.19
  1.5 0.1 eq.104
  1.6 0.1 fusion.56
  1.7 0.1 mul.158
  1.8 0.1 mul.159
  1.9 0.1 fusion.57
  2.0 0.1 eq.108
  2.1 0.1 eq.109
  2.2 0.1 eq.101
  2.3 0.8 copy.20
  3.1 0.8 copy.18
  3.8 0.8 copy.17
  4.6 0.1 eq.94
  4.7 0.1 fusion.55
  4.8 0.1 mul.142
  4.9 0.1 mul.143
  5.0 0.1 fusion.58
  5.1 0.1 eq.98
  5.2 0.1 eq.99
  5.3 1.0 fusion.32
  6.4 0.8 reduce
  7.1 0.7 fusion.63
  7.9 1.2 convolution_convert_fusion.1
  9.0 0.1 broadcast_in_dim.41
  9.2 2.1 broadcast_in_dim.42
  11.3 12.4 %all-to-all-start.3 = ((bf16[64,6,3584]{2,1,0:T(8,128)(2,1)}), bf16[64,6,3584]{2,1,0:T(8,128)(2,1)}, u32[]{:S(2)}, u32[]{:S(2)}) async-start(bf16[64,6,3584]{2,1,0:T(8,128)(2,1)} %bitcast.69), calls=%async_computation.3 | async-start | bytes 7340032 | tf_op jit(solution)/shard_map/all_to_all | solution.py:87
  23.7 1.9 collective-permute-start
  25.6 60.0 %collective-permute-done = bf16[1,16,3584]{2,1,0:T(8,128)(2,1)S(1)} collective-permute-done((bf16[1,16,3584]{2,1,0:T(8,128)(2,1)S(1)}, bf16[1,16,3584]{2,1,0:T(8,128)(2,1)S(1)}, u32[]{:S(2)}, u32[]{:S(2)}) %collective-permute-start) | collective-permute-done | bytes 114720 | tf_op jit(solution)/shard_map/ppermute | solution.py:15
  85.6 0.1 fusion.29
  85.7 0.3 convolution_convert_fusion.3
  86.0 0.1 broadcast_in_dim.16
  86.2 21.2 %all-to-all-done.3 = bf16[64,6,3584]{2,1,0:T(8,128)(2,1)} async-done(((bf16[64,6,3584]{2,1,0:T(8,128)(2,1)}), bf16[64,6,3584]{2,1,0:T(8,128)(2,1)}, u32[]{:S(2)}, u32[]{:S(2)}) %all-to-all-start.3) | async-done | bytes 2752544 | tf_op jit(solution)/shard_map/all_to_all | solution.py:87
  107.4 2.2 broadcast_in_dim.17
  109.5 11.1 %all-to-all-start = ((bf16[64,6,3584]{2,1,0:T(8,128)(2,1)}), bf16[64,6,3584]{2,1,0:T(8,128)(2,1)}, u32[]{:S(2)}, u32[]{:S(2)}) async-start(bf16[64,6,3584]{2,1,0:T(8,128)(2,1)} %bitcast.70), calls=%async_computation | async-start | bytes 7340032 | tf_op jit(solution)/shard_map/all_to_all | solution.py:86
  120.6 1.9 collective-permute-start.1
  122.5 2.3 collective-permute-done.1
  124.9 0.3 convolution_convert_fusion.2
  125.2 0.1 broadcast_in_dim.19
  125.3 81.5 %all-to-all-done = bf16[64,6,3584]{2,1,0:T(8,128)(2,1)} async-done(((bf16[64,6,3584]{2,1,0:T(8,128)(2,1)}), bf16[64,6,3584]{2,1,0:T(8,128)(2,1)}, u32[]{:S(2)}, u32[]{:S(2)}) %all-to-all-start) | async-done | bytes 2752544 | tf_op jit(solution)/shard_map/all_to_all | solution.py:86
  206.8 2.1 broadcast_in_dim.40
  208.9 5.7 %all-to-all-start.2 = ((bf16[64,6,3584]{2,1,0:T(8,128)(2,1)}), bf16[64,6,3584]{2,1,0:T(8,128)(2,1)}, u32[]{:S(2)}, u32[]{:S(2)}) async-start(bf16[64,6,3584]{2,1,0:T(8,128)(2,1)} %bitcast.71), calls=%async_computation.2 | async-start | bytes 7340032 | tf_op jit(solution)/shard_map/all_to_all | solution.py:88
  214.6 5.5 %reshape.225 = bf16[384,3584]{1,0:T(8,128)(2,1)} reshape(bf16[64,6,3584]{2,1,0:T(8,128)(2,1)} %all-to-all-done) | data formatting | bytes 5505024 | tf_op jit(solution)/shard_map/reshape | solution.py:90
  220.1 2.7 fusion.19
  222.9 6.4 %convolution_convert_fusion = bf16[384,3584]{1,0:T(8,128)(2,1)} fusion(bf16[384,3584]{1,0:T(8,128)(2,1)} %reshape.225, bf16[1,128,3584]{2,1,0:T(8,128)(2,1)S(1)} %copy-done.2, bf16[1,3584,128]{2,1,0:T(8,128)(2,1)S(1)} %copy-done, f32[384,128]{1,0:T(8,128)S(1)} %fusion.19), kind=kOutput, calls=%fused_computation.4 | convolution fusion | flops 706314240 | bytes 7536640 | tf_op jit(solution)/shard_map/dot_general | solution.py:94
  229.2 5.4 %reshape.226 = bf16[64,6,3584]{2,1,0:T(8,128)(2,1)} reshape(bf16[384,3584]{1,0:T(8,128)(2,1)} %convolution_convert_fusion) | data formatting | bytes 5505024 | tf_op jit(solution)/shard_map/reshape | solution.py:109
  234.6 62.8 %all-to-all-done.2 = bf16[64,6,3584]{2,1,0:T(8,128)(2,1)} async-done(((bf16[64,6,3584]{2,1,0:T(8,128)(2,1)}), bf16[64,6,3584]{2,1,0:T(8,128)(2,1)}, u32[]{:S(2)}, u32[]{:S(2)}) %all-to-all-start.2) | async-done | bytes 2752544 | tf_op jit(solution)/shard_map/all_to_all | solution.py:88
  297.4 7.2 %all-to-all-start.1 = ((bf16[64,6,3584]{2,1,0:T(8,128)(2,1)}), bf16[64,6,3584]{2,1,0:T(8,128)(2,1)}, u32[]{:S(2)}, u32[]{:S(2)}) async-start(bf16[64,6,3584]{2,1,0:T(8,128)(2,1)} %reshape.226), calls=%async_computation.1 | async-start | bytes 7340032 | tf_op jit(solution)/shard_map/all_to_all | solution.py:113
  304.6 5.5 %reshape.231 = bf16[384,3584]{1,0:T(8,128)(2,1)} reshape(bf16[64,6,3584]{2,1,0:T(8,128)(2,1)} %all-to-all-done.3) | data formatting | bytes 5505024 | tf_op jit(solution)/shard_map/reshape | solution.py:97
  310.1 2.6 fusion.17
  312.7 5.5 %reshape.229 = bf16[384,3584]{1,0:T(8,128)(2,1)} reshape(bf16[64,6,3584]{2,1,0:T(8,128)(2,1)} %all-to-all-done.2) | data formatting | bytes 5505024 | tf_op jit(solution)/shard_map/reshape | solution.py:101
  318.2 2.6 fusion.8
  320.8 7.2 %fusion.7 = f32[384,3584]{1,0:T(8,128)} fusion(f32[384,128]{1,0:T(8,128)S(1)} %fusion.8, bf16[384,3584]{1,0:T(8,128)(2,1)} %reshape.231, bf16[1,3584,128]{2,1,0:T(8,128)(2,1)S(1)} %copy-done, bf16[1,3584,128]{2,1,0:T(8,128)(2,1)S(1)} %copy-done.1, f32[384,128]{1,0:T(8,128)S(1)} %fusion.17), kind=kOutput, calls=%fused_computation.18 | convolution fusion | flops 705134592 | bytes 10485760 | tf_op jit(solution)/shard_map/dot_general | solution.py:106
  328.0 5.0 %fusion = bf16[384,3584]{1,0:T(8,128)(2,1)} fusion(f32[384,3584]{1,0:T(8,128)} %fusion.7, bf16[1,3584,128]{2,1,0:T(8,128)(2,1)S(1)} %copy-done, f32[384,128]{1,0:T(8,128)S(1)} %fusion.8, f32[384,128]{1,0:T(8,128)S(1)} %fusion.17), kind=kOutput, calls=%fused_computation.3 | convolution fusion | flops 355368960 | bytes 9568256 | tf_op jit(solution)/shard_map/dot_general | solution.py:107
  333.0 5.4 %reshape.232 = bf16[64,6,3584]{2,1,0:T(8,128)(2,1)} reshape(bf16[384,3584]{1,0:T(8,128)(2,1)} %fusion) | data formatting | bytes 5505024 | tf_op jit(solution)/shard_map/reshape | solution.py:110
  338.4 51.3 %all-to-all-done.1 = bf16[64,6,3584]{2,1,0:T(8,128)(2,1)} async-done(((bf16[64,6,3584]{2,1,0:T(8,128)(2,1)}), bf16[64,6,3584]{2,1,0:T(8,128)(2,1)}, u32[]{:S(2)}, u32[]{:S(2)}) %all-to-all-start.1) | async-done | bytes 2752544 | tf_op jit(solution)/shard_map/all_to_all | solution.py:113
  389.7 9.6 %all-to-all-start.4 = ((bf16[64,6,3584]{2,1,0:T(8,128)(2,1)}), bf16[64,6,3584]{2,1,0:T(8,128)(2,1)}, u32[]{:S(2)}, u32[]{:S(2)}) async-start(bf16[64,6,3584]{2,1,0:T(8,128)(2,1)} %reshape.232), calls=%async_computation.4 | async-start | bytes 7340032 | tf_op jit(solution)/shard_map/all_to_all | solution.py:114
  399.4 2.9 convert_reduce_fusion.1
  402.2 0.1 reshape.227
  402.4 80.9 %all-to-all-done.4 = bf16[64,6,3584]{2,1,0:T(8,128)(2,1)} async-done(((bf16[64,6,3584]{2,1,0:T(8,128)(2,1)}), bf16[64,6,3584]{2,1,0:T(8,128)(2,1)}, u32[]{:S(2)}, u32[]{:S(2)}) %all-to-all-start.4) | async-done | bytes 2752544 | tf_op jit(solution)/shard_map/all_to_all | solution.py:114
  483.2 2.9 convert_reduce_fusion
  486.1 0.1 reshape.233
  486.2 1.3 fusion.33
  487.5 1.8 fusion.2
  489.3 1.4 fusion.43
  (23 shorter events, 0.2 us)
Async XLA Ops:
  0.6 222.2 %copy-start = (bf16[1,3584,128]{2,1,0:T(8,128)(2,1)S(1)}, bf16[1,3584,128]{2,1,0:T(8,128)(2,1)}, u32[]{:S(2)}) copy-start(bf16[1,3584,128]{2,1,0:T(8,128)(2,1)} %param.16) | copy-start | bytes 2752516
  6.4 1.5 copy-start.5
  7.1 78.6 %copy-start.4 = (f32[3584]{0:T(1024)}, f32[3584]{0:T(1024)S(1)}, u32[]{:S(2)}) copy-start(f32[3584]{0:T(1024)S(1)} %reduce) | copy-start | bytes 43012
  11.3 12.4 %copy-start.6 = (bf16[1,16,3584]{2,1,0:T(8,128)(2,1)S(1)}, bf16[1,16,3584]{2,1,0:T(8,128)(2,1)}, u32[]{:S(2)}) copy-start(bf16[1,16,3584]{2,1,0:T(8,128)(2,1)} %param.11) | copy-start | bytes 344068
  11.3 96.1 %all-to-all-start.3 = ((bf16[64,6,3584]{2,1,0:T(8,128)(2,1)}), bf16[64,6,3584]{2,1,0:T(8,128)(2,1)}, u32[]{:S(2)}, u32[]{:S(2)}) async-start(bf16[64,6,3584]{2,1,0:T(8,128)(2,1)} %bitcast.69), calls=%async_computation.3 | async-start | bytes 7340032 | tf_op jit(solution)/shard_map/all_to_all | solution.py:87
  23.7 61.9 %collective-permute-start = (bf16[1,16,3584]{2,1,0:T(8,128)(2,1)S(1)}, bf16[1,16,3584]{2,1,0:T(8,128)(2,1)S(1)}, u32[]{:S(2)}, u32[]{:S(2)}) collective-permute-start(bf16[1,16,3584]{2,1,0:T(8,128)(2,1)S(1)} %copy-done.6), channel_id=1, source_target_pairs={{448,0},{0,64},{64,128},{128,192},{192,256},{256,320},{320,384},{3... | collective-permute-start | bytes 344072 | tf_op jit(solution)/shard_map/ppermute | solution.py:15
  109.5 11.1 %copy-start.7 = (bf16[1,16,3584]{2,1,0:T(8,128)(2,1)S(1)}, bf16[1,16,3584]{2,1,0:T(8,128)(2,1)}, u32[]{:S(2)}) copy-start(bf16[1,16,3584]{2,1,0:T(8,128)(2,1)} %param.12) | copy-start | bytes 344068
  109.5 97.3 %all-to-all-start = ((bf16[64,6,3584]{2,1,0:T(8,128)(2,1)}), bf16[64,6,3584]{2,1,0:T(8,128)(2,1)}, u32[]{:S(2)}, u32[]{:S(2)}) async-start(bf16[64,6,3584]{2,1,0:T(8,128)(2,1)} %bitcast.70), calls=%async_computation | async-start | bytes 7340032 | tf_op jit(solution)/shard_map/all_to_all | solution.py:86
  120.6 4.3 collective-permute-start.1
  208.9 88.5 %all-to-all-start.2 = ((bf16[64,6,3584]{2,1,0:T(8,128)(2,1)}), bf16[64,6,3584]{2,1,0:T(8,128)(2,1)}, u32[]{:S(2)}, u32[]{:S(2)}) async-start(bf16[64,6,3584]{2,1,0:T(8,128)(2,1)} %bitcast.71), calls=%async_computation.2 | async-start | bytes 7340032 | tf_op jit(solution)/shard_map/all_to_all | solution.py:88
  214.6 5.5 %copy-start.1 = (bf16[1,3584,128]{2,1,0:T(8,128)(2,1)S(1)}, bf16[1,3584,128]{2,1,0:T(8,128)(2,1)}, u32[]{:S(2)}) copy-start(bf16[1,3584,128]{2,1,0:T(8,128)(2,1)} %param.15) | copy-start | bytes 2752516
  220.1 2.7 copy-start.2
  297.4 92.3 %all-to-all-start.1 = ((bf16[64,6,3584]{2,1,0:T(8,128)(2,1)}), bf16[64,6,3584]{2,1,0:T(8,128)(2,1)}, u32[]{:S(2)}, u32[]{:S(2)}) async-start(bf16[64,6,3584]{2,1,0:T(8,128)(2,1)} %reshape.226), calls=%async_computation.1 | async-start | bytes 7340032 | tf_op jit(solution)/shard_map/all_to_all | solution.py:113
  389.7 93.5 %all-to-all-start.4 = ((bf16[64,6,3584]{2,1,0:T(8,128)(2,1)}), bf16[64,6,3584]{2,1,0:T(8,128)(2,1)}, u32[]{:S(2)}, u32[]{:S(2)}) async-start(bf16[64,6,3584]{2,1,0:T(8,128)(2,1)} %reshape.232), calls=%async_computation.4 | async-start | bytes 7340032 | tf_op jit(solution)/shard_map/all_to_all | solution.py:114
  402.3 83.9 %copy-start.3 = (bf16[1,16,3584]{2,1,0:T(8,128)(2,1)S(1)}, bf16[1,16,3584]{2,1,0:T(8,128)(2,1)}, u32[]{:S(2)}) copy-start(bf16[1,16,3584]{2,1,0:T(8,128)(2,1)} %param.13) | copy-start | bytes 344068
where the time goes:
time: 492 us; the launch traced here: 491 us
  waiting for transfers between devices  360 us (73%)
  starting transfers between devices  49.8 us (10%)
  local copies, waits for them, and re-layouts  38.4 us (8%)
  matrix products  31.4 us (6%)
  other arithmetic  10.2 us (2%)
    all_to_all x1, waiting for transfers between devices, local(): lax.all_to_all(sent_rows, 'expert', split_axis=0, concat_axis=0, tiled=True)  81.5 us
    all_to_all x1, waiting for transfers between devices, local(): lax.all_to_all(grad_part, 'expert', split_axis=0, concat_axis=0, tiled=True)  80.9 us
    all_to_all x1, waiting for transfers between devices, local(): lax.all_to_all(sent_cot, 'expert', split_axis=0, concat_axis=0, tiled=True)  62.8 us
    ppermute x2, waiting for transfers between devices, shifted(): return lax.ppermute(block, axis, route)  62.3 us
    all_to_all x1, waiting for transfers between devices, local(): lax.all_to_all(forward_part, 'expert', split_axis=0, concat_axis=0, tiled...  51.3 us
    all_to_all x1, waiting for transfers between devices, local(): lax.all_to_all(sent_back, 'expert', split_axis=0, concat_axis=0, tiled=True)  21.2 us
    all_to_all x1, starting transfers between devices, local(): lax.all_to_all(sent_back, 'expert', split_axis=0, concat_axis=0, tiled=True)  12.4 us
    all_to_all x1, starting transfers between devices, local(): lax.all_to_all(sent_rows, 'expert', split_axis=0, concat_axis=0, tiled=True)  11.1 us
  transfers between devices with their start and end apart: 7, of which 7 were waited for; matrix products, arithmetic and copies ran while one was open for 12% of the time, Pallas kernels for 0%

commit v1 on v0

v1 whole, which is shorter than its diff:
```python
import functools

import jax
import jax.numpy as jnp
import numpy as np
from jax import lax
from jax.experimental import pallas as pl
from jax.experimental.pallas import tpu as pltpu
from jax.sharding import PartitionSpec as P

EPS = 1e-06
SIDE = 4
MOST = 6
BF16 = jnp.bfloat16
F32 = jnp.float32


def dot(a, b):
    return lax.dot_general(a, b, (((1,), (0,)), ((), ())), preferred_element_type=F32)


def dot_t(a, b):
    return lax.dot_general(a, b, (((1,), (1,)), ((), ())), preferred_element_type=F32)


def constants(tokens):
    per = SIDE * MOST
    r = np.arange(4 * per)
    half, chunk, src, place = r // (2 * per), r // per % 2, r // MOST % SIDE, r % MOST
    t = np.arange(SIDE * tokens) // tokens
    row_lane = np.broadcast_to((half * MOST + place)[:, None], (4 * per, 128)).astype(np.int32)
    mask = np.stack([(src[:, None] == t[None, :]) & (chunk == c)[:, None] for c in range(2)])
    pick = np.zeros((2, SIDE * per, SIDE * 2 * per))
    for y in range(SIDE):
        for c in range(2):
            for i in range(per):
                pick[c, y * per + i, (y * 2 + c) * per + i] = 1
    lane = np.arange(128)
    lane_expert = np.where(lane % 64 < 48, lane % 64 // MOST, -1).astype(np.int32)
    lane_place = (lane % 64 % MOST).astype(np.float32)
    before = (np.arange(tokens)[:, None] > np.arange(tokens)[None, :]).astype(np.float32)
    return (
        jnp.asarray(row_lane),
        jnp.asarray(mask, BF16),
        jnp.asarray(np.swapaxes(mask, 1, 2), BF16),
        jnp.asarray(pick, BF16),
        jnp.asarray(np.swapaxes(pick, 1, 2), BF16),
        jnp.asarray(np.broadcast_to(lane_expert, (tokens, 128))),
        jnp.asarray(np.broadcast_to(lane_place, (tokens, 128))),
        jnp.asarray(before, BF16),
    )


N_SEMS = 72


def kernel(
    acts, grads, saved_ref, gain_ref, gate_w, up_w, down_w, f_routes, f_gates, b_routes, b_gates,
    row_lane, mask, mask_t, pick, pick_t, lane_expert, lane_place, before,
    out_ref, din_ref,
    in_buf, zbuf, tab, ysend, yrecv, xbuf, w1, wd, part, psend, precv, act, dgu,
    mine, rsopp, rsrecv, rssend, rsin, ypack, yret, zsend, zret, own,
    send_sem, recv_sem, copy_sem,
):
    tokens, width = saved_ref.shape[1], saved_ref.shape[2]
    half_d, chunk = width // 2, width // 4
    rows = xbuf.shape[1] * xbuf.shape[2]
    block = xbuf.shape[2]
    hb = block // 2
    hid = wd.shape[0] // 2
    pipe = lax.axis_index("pipe")
    n_pipe = lax.axis_size("pipe")
    me = lax.axis_index("expert")
    z, y, x = me // (SIDE * SIDE), me // SIDE % SIDE, me % SIDE
    h, yl = y // 2, y % 2
    other = 1 - yl

    def at(zz, yy, xx):
        return (pipe, (zz * SIDE + yy) * SIDE + xx)

    ahead, behind = (lax.rem(pipe + 1, n_pipe), me), (lax.rem(pipe + n_pipe - 1, n_pipe), me)
    zs = [lax.rem(z + k, SIDE) for k in range(SIDE)]
    ys = [lax.rem(y + k, SIDE) for k in range(SIDE)]
    xr, xo, xl = (lax.rem(x + k, SIDE) for k in (1, 2, 3))
    right, left = at(z, y, xr), at(z, y, xl)
    mate = at(z, h * 2 + other, x)
    z_peers = [at(zs[k], y, x) for k in (1, 2, 3)]
    y_peers = [at(z, ys[k], x) for k in (1, 2, 3)]

    barrier = pltpu.get_barrier_semaphore()
    peers = [ahead, behind, right, left] + z_peers + y_peers
    for p in peers:
        pl.semaphore_signal(barrier, inc=1, device_id=p, device_id_type=pl.DeviceIdType.MESH)
    pl.semaphore_wait(barrier, len(peers))

    started = []

    def send(src, dst, to):
        i = len(started)
        c = pltpu.make_async_remote_copy(
            src_ref=src, dst_ref=dst, send_sem=send_sem.at[i], recv_sem=recv_sem.at[i],
            device_id=to, device_id_type=pl.DeviceIdType.MESH,
        )
        c.start()
        started.append(c)
        return c

    local = []

    def fetch(src, dst):
        c = pltpu.make_async_copy(src, dst, copy_sem.at[len(local)])
        c.start()
        local.append(c)
        return c

    F, B, C = 0, 1, 2

    c_acts = send(acts.at[0], in_buf, ahead)
    c_grads = send(grads.at[0], zbuf.at[C, z], behind)

    lane = lax.broadcasted_iota(jnp.int32, (tokens, 128), 1)
    is_f = lane < 64
    le = lane_expert[...]
    fr, fg, br, bg = f_routes[0], f_gates[0], b_routes[0], b_gates[0]
    first = le == jnp.where(is_f, fr[:, 0:1], br[:, 0:1])
    second = le == jnp.where(is_f, fr[:, 1:2], br[:, 1:2])
    weight = jnp.where(first, jnp.where(is_f, fg[:, 0:1], bg[:, 0:1]), 0.0)
    weight = weight + jnp.where(second, jnp.where(is_f, fg[:, 1:2], bg[:, 1:2]), 0.0)
    named = jnp.where(first | second, 1.0, 0.0)
    earlier = dot(before[...], named.astype(BF16))
    tab[z] = jnp.where(earlier == lane_place[...], weight, 0.0)
    c_tab = [send(tab.at[z], tab.at[z], p) for p in z_peers]

    def scale_of(v):
        return lax.rsqrt(jnp.mean(v * v, axis=-1, keepdims=True) + EPS)

    def z_spread(a):
        return [send(zbuf.at[a, z], zbuf.at[a, z], p) for p in z_peers]

    gain = gain_ref[...]
    v = saved_ref[0].astype(F32)
    zbuf[B, z] = (v * scale_of(v) * gain).astype(BF16)
    cz = {B: z_spread(B)}

    def d_half(k):
        return pl.ds(pl.multiple_of(k * half_d, half_d), half_d)

    def hidden(k):
        return pl.ds(pl.multiple_of(k * hid, hid), hid)

    f_gu = [fetch(gate_w.at[0, d_half(yl), :], w1.at[yl, :, 0:hid]),
            fetch(up_w.at[0, d_half(yl), :], w1.at[yl, :, hid:2 * hid])]
    f_d = fetch(down_w.at[0, :, d_half(yl)], wd.at[hidden(yl), :])
    c_gu = [send(gate_w.at[0, d_half(other), :], w1.at[yl, :, 0:hid], mate),
            send(up_w.at[0, d_half(other), :], w1.at[yl, :, hid:2 * hid], mate)]

    c_acts.wait_recv()
    v = in_buf[...].astype(F32)
    zbuf[F, z] = (v * scale_of(v) * gain).astype(BF16)
    cz[F] = z_spread(F)
    c_grads.wait_recv()
    cz[C] = z_spread(C)

    for c in c_tab:
        c.wait_recv()
    table = tab[...].reshape(SIDE * tokens, 128)
    lane96 = lax.broadcasted_iota(jnp.int32, row_lane.shape, 1)
    q = [jnp.where(lane96 == row_lane[...] + (2 * MOST * z + 64 * d), 1.0, 0.0).astype(BF16) for d in (0, 1)]
    chosen = jnp.where(table > 0, 1.0, 0.0).astype(BF16)
    selects = [dot_t(q[d], chosen).astype(BF16) for d in (0, 1)]

    def y_spread(a):
        for c in cz[a]:
            c.wait_recv()
        s = selects[0 if a == F else 1]
        s = [s * mask[c] for c in range(2)]
        for k in range(2):
            got = None
            for c in range(2):
                col = k * half_d + c * chunk
                part_c = dot(s[c], zbuf[a, :, :, col:col + chunk].reshape(SIDE * tokens, chunk))
                got = part_c if got is None else got + part_c
            got = got.astype(BF16)
            ysend[a, k, 0] = got[:2 * SIDE * MOST]
            ysend[a, k, 1] = got[2 * SIDE * MOST:]
        yrecv[a, y] = ysend[a, yl, h]
        return [
            send(ysend.at[a, ys[k] % 2, ys[k] // 2], yrecv.at[a, y], y_peers[k - 1])
            for k in (1, 2, 3)
        ]

    def x_spread(a, cy):
        for c in cy:
            c.wait_recv()
        packed = yrecv[a].reshape(SIDE * yrecv.shape[2], chunk)
        for c in range(2):
            xbuf[a, x, :, c * chunk:(c + 1) * chunk] = dot(pick[c], packed).astype(BF16)
        return [send(xbuf.at[a, x], xbuf.at[a, x], right), send(xbuf.at[a, x], xbuf.at[a, x], left)]

    def x_forward(a, cx):
        cx[0].wait_recv()
        one = send(xbuf.at[a, xl, 0:hb], xbuf.at[a, xl, 0:hb], right)
        cx[1].wait_recv()
        two = send(xbuf.at[a, xr, hb:block], xbuf.at[a, xr, hb:block], left)
        return [one, two]

    def gathered(a, cf):
        for c in cf:
            c.wait_recv()
        return xbuf[a].reshape(rows, half_d)

    cy = {B: y_spread(B)}
    cy[F] = y_spread(F)
    cx = {B: x_spread(B, cy[B])}
    cy[C] = y_spread(C)
    cx[F] = x_spread(F, cy[F])
    c_d = send(down_w.at[0, :, d_half(other)], wd.at[hidden(yl), :], mate)
    cf = {B: x_forward(B, cx[B])}
    cx[C] = x_spread(C, cy[C])
    cf[F] = x_forward(F, cx[F])

    for c in f_gu:
        c.wait()
    for c in c_gu:
        c.wait_recv()

    def gate_up(a):
        r = gathered(a, cf[a])
        psend[a] = dot(r, w1[other]).astype(BF16)
        c = send(psend.at[a], precv.at[a], mate)
        part[a] = dot(r, w1[yl])
        return c

    cp = {B: gate_up(B)}
    cf[C] = x_forward(C, cx[C])
    cp[F] = gate_up(F)

    cp[F].wait_recv()
    gu = part[F] + precv[F].astype(F32)
    gate, up = gu[:, :hid], gu[:, hid:]
    act[yl] = (gate * jax.nn.sigmoid(gate) * up).astype(BF16)
    c_act = send(act.at[yl], act.at[yl], mate)
    f_d.wait()
    c_d.wait_recv()

    r = gathered(C, cf[C])
    psend[C, :, 0:hid] = dot_t(r, wd[hidden(other), :]).astype(BF16)
    cp[C] = send(psend.at[C, :, 0:hid], precv.at[C, :, 0:hid], mate)
    d_part = dot_t(r, wd[hidden(yl), :])

    def reduce_one(d, block_of):
        rsopp[d] = block_of(xo).astype(BF16)
        one = send(rsopp.at[d, 0:hb], rsrecv.at[d, 0], right)
        two = send(rsopp.at[d, hb:block], rsrecv.at[d, 1], left)
        mine[d, 0] = block_of(xr)
        mine[d, 1] = block_of(xl)
        mine[d, 2] = block_of(x)
        return [one, two]

    def reduce_two(d, cr):
        cr[0].wait_recv()
        rssend[d, 0, 0:hb] = (mine[d, 0, 0:hb] + rsrecv[d, 0].astype(F32)).astype(BF16)
        rssend[d, 0, hb:block] = mine[d, 0, hb:block].astype(BF16)
        one = send(rssend.at[d, 0], rsin.at[d, 0], right)
        cr[1].wait_recv()
        rssend[d, 1, hb:block] = (mine[d, 1, hb:block] + rsrecv[d, 1].astype(F32)).astype(BF16)
        rssend[d, 1, 0:hb] = mine[d, 1, 0:hb].astype(BF16)
        two = send(rssend.at[d, 1], rsin.at[d, 1], left)
        return [one, two]

    def y_return(d, cr):
        for c in cr:
            c.wait_recv()
        total = mine[d, 2] + rsin[d, 0].astype(F32) + rsin[d, 1].astype(F32)
        total = total.astype(BF16)
        packed = dot(pick_t[0], total[:, :chunk]) + dot(pick_t[1], total[:, chunk:])
        packed = packed.astype(BF16).reshape(ypack.shape[1:])
        ypack[d] = packed
        yret[d, yl, h] = ypack[d, y]
        return [send(ypack.at[d, ys[k]], yret.at[d, yl, h], y_peers[k - 1]) for k in (1, 2, 3)]

    w_hi = table.astype(BF16)
    w_lo = (table - w_hi.astype(F32)).astype(BF16)

    def z_return(d, cr):
        for c in cr:
            c.wait_recv()
        hi, lo = dot_t(w_hi, q[d]).astype(BF16), dot_t(w_lo, q[d]).astype(BF16)
        for k in range(2):
            slots = yret[d, k].reshape(2 * yret.shape[3], chunk)
            for c in range(2):
                col = k * half_d + c * chunk
                m = mask_t[c]
                got = dot(hi * m, slots) + dot(lo * m, slots)
                own[d, :, :, col:col + chunk] = got.reshape(SIDE, tokens, chunk)
        zsend[d] = own[d].astype(BF16)
        return [send(zsend.at[d, zs[k]], zret.at[d, k - 1], z_peers[k - 1]) for k in (1, 2, 3)]

    def total_of(d, cr):
        s = own[d, z]
        for k, c in enumerate(cr):
            c.wait_recv()
            s = s + zret[d, k].astype(F32)
        return s

    c_act.wait_recv()

    def f_block(k):
        return dot(act[0, pl.ds(pl.multiple_of(k * block, block), block), :], wd[0:hid, :]) + dot(
            act[1, pl.ds(pl.multiple_of(k * block, block), block), :], wd[hid:2 * hid, :])

    cr_f = reduce_one(0, f_block)

    cp[B].wait_recv()
    gu = part[B] + precv[B].astype(F32)
    gate, up = gu[:, :hid], gu[:, hid:]
    sigma = jax.nn.sigmoid(gate)
    by_gate = up * sigma * (1.0 + gate * (1.0 - sigma))
    by_up = gate * sigma
    cp[C].wait_recv()
    d_act = d_part + precv[C, :, 0:hid].astype(F32)
    dgu[yl, :, 0:hid] = (d_act * by_gate).astype(BF16)
    dgu[yl, :, hid:2 * hid] = (d_act * by_up).astype(BF16)
    c_dgu = send(dgu.at[yl], dgu.at[yl], mate)

    cr_f = reduce_two(0, cr_f)

    def b_block(k):
        at_k = pl.ds(pl.multiple_of(k * block, block), block)
        return dot_t(dgu[0, at_k, :], w1[0]) + dot_t(dgu[1, at_k, :], w1[1])

    c_dgu.wait_recv()
    cr_b = reduce_one(1, b_block)
    cr_f = y_return(0, cr_f)
    cr_b = reduce_two(1, cr_b)
    cr_f = z_return(0, cr_f)
    cr_b = y_return(1, cr_b)

    out_ref[0] = (in_buf[...].astype(F32) + total_of(0, cr_f)).astype(BF16)

    cr_b = z_return(1, cr_b)
    v = saved_ref[0].astype(F32)
    scale = scale_of(v)
    dn = total_of(1, cr_b) * gain
    d_in = scale * dn - v * (scale * scale * scale) * jnp.mean(dn * v, axis=-1, keepdims=True)
    din_ref[0] = (zbuf[C, z].astype(F32) + d_in).astype(BF16)

    for c in started:
        c.wait_send()


def local(*args):
    held_acts = args[0]
    tokens, width = held_acts.shape[1:]
    hid = args[4].shape[2]
    per = SIDE * MOST
    block = SIDE * per
    rows = SIDE * block
    half_d, chunk = width // 2, width // 4
    consts = constants(tokens)
    vmem, hbm = pl.BlockSpec(memory_space=pltpu.VMEM), pl.BlockSpec(memory_space=pl.ANY)
    out = jax.ShapeDtypeStruct((1, tokens, width), BF16)
    V = pltpu.VMEM
    return pl.pallas_call(
        kernel,
        out_shape=(out, out),
        in_specs=[hbm, hbm, vmem, vmem, hbm, hbm, hbm] + [vmem] * (4 + len(consts)),
        out_specs=(vmem, vmem),
        scratch_shapes=[
            V((tokens, width), BF16),
            V((3, SIDE, tokens, width), BF16),
            V((SIDE, tokens, 128), F32),
            V((3, 2, 2, 2 * per, chunk), BF16),
            V((3, SIDE, 2 * per, chunk), BF16),
            V((3, SIDE, block, half_d), BF16),
            V((2, half_d, 2 * hid), BF16),
            V((2 * hid, half_d), BF16),
            V((2, rows, 2 * hid), F32),
            V((3, rows, 2 * hid), BF16),
            V((3, rows, 2 * hid), BF16),
            V((2, rows, hid), BF16),
            V((2, rows, 2 * hid), BF16),
            V((2, 3, block, half_d), F32),
            V((2, block, half_d), BF16),
            V((2, 2, block // 2, half_d), BF16),
            V((2, 2, block, half_d), BF16),
            V((2, 2, block, half_d), BF16),
            V((2, SIDE, 2 * per, chunk), BF16),
            V((2, 2, 2, 2 * per, chunk), BF16),
            V((2, SIDE, tokens, width), BF16),
            V((2, SIDE - 1, tokens, width), BF16),
            V((2, SIDE, tokens, width), F32),
            pltpu.SemaphoreType.DMA((N_SEMS,)),
            pltpu.SemaphoreType.DMA((N_SEMS,)),
            pltpu.SemaphoreType.DMA((3,)),
        ],
        compiler_params=pltpu.CompilerParams(
            collective_id=0, has_side_effects=True, vmem_limit_bytes=58 * 1024 * 1024
        ),
    )(*args, *consts)


def solution(mesh):
    return jax.shard_map(
        local,
        mesh=mesh,
        in_specs=(
            P("pipe", "expert", None),
            P("pipe", "expert", None),
            P("pipe", "expert", None),
            P("pipe", None),
            P("pipe", None, "expert"),
            P("pipe", None, "expert"),
            P("pipe", "expert", None),
            P("pipe", "expert", None),
            P("pipe", "expert", None),
            P("pipe", "expert", None),
            P("pipe", "expert", None),
        ),
        out_specs=(P("pipe", "expert", None), P("pipe", "expert", None)),
        check_vma=False,
    )
```

time: 492 us -> 139 us (0.28)
  the two profiles are of different devices: /device:TPU:128 before, /device:TPU:18 now
where the time goes in v1:
time: 139 us
  Pallas kernels  131 us (94%)
  local copies, waits for them, and re-layouts  6.9 us (5%)
    pallas_call x1, Pallas kernels, local(): pl.pallas_call(kernel, out_shape=(out, out), in_specs=[hbm, hbm, vmem, vm...  131 us
    unnamed x18, local copies, waits for them, and re-layouts  5.7 us

profile of v1, /device:TPU:18, one launch (start us, length us, event | category | flops | bytes accessed | tf_op | source)
XLA Modules:
  0.0 138.8 jit_solution(2047848450986140794)
XLA Ops:
  0.6 0.0 copy-start.1
  0.6 1.4 copy.21.f_routes
  2.0 0.0 copy-done.1
  2.0 0.0 copy-start.2
  2.0 0.7 copy.22.f_gates
  2.7 0.0 copy-done.2
  2.7 0.0 copy-start.3
  2.7 0.7 copy.23.b_routes
  3.4 0.0 copy-done.3
  3.4 0.0 copy-start.5
  3.4 0.7 copy.24.b_gates
  4.0 0.0 copy-done.5
  4.0 0.0 copy-start.4
  4.1 0.6 jit_solution_.6.lane_expert
  4.6 0.1 copy-done.4
  4.7 0.6 jit_solution_.7.lane_place
  5.3 131.2 %shard_map.194 = (bf16[1,16,3584]{2,1,0:T(8,128)(2,1)}, bf16[1,16,3584]{2,1,0:T(8,128)(2,1)}) custom-call(bf16[1,16,3584]{2,1,0:T(8,128)(2,1)} %acts.1, bf16[1,16,3584]{2,1,0:T(8,128)(2,1)} %grads.1, bf16[1,16,3584]{2,1,0:T(8,128)(2,1)} %saved_ref.1, f32[1,3584]{1,0:T(1,128)} %gain_ref.1, bf16[1,3584,128]{2,1,0:T(8,128)(2,1)} %gate_w.1, ...), custom_call_target="tpu_custom_call" | custom-call | tf_op jit(solution)/shard_map/pallas_call | solution.py:364
  136.5 0.0 copy-start
  136.5 1.6 %copy.27 = bf16[1,16,3584]{2,1,0:T(8,128)(2,1)} copy(bf16[1,16,3584]{2,1,0:T(8,128)(2,1)} %get-tuple-element.4) | data formatting | bytes 229376
  138.1 0.0 copy-done
  138.1 0.6 copy.28
Async XLA Ops:
  0.6 1.4 copy-start.1
  2.0 0.7 copy-start.2
  2.7 0.7 copy-start.3
  3.4 0.7 copy-start.5
  4.0 0.7 copy-start.4
  136.5 1.6 %copy-start = (bf16[1,16,3584]{2,1,0:T(8,128)(2,1)S(1)}, bf16[1,16,3584]{2,1,0:T(8,128)(2,1)}, u32[]{:S(2)}) copy-start(bf16[1,16,3584]{2,1,0:T(8,128)(2,1)} %get-tuple-element.5) | copy-start | bytes 344068

commit v2 on v1

v2 whole, which is shorter than its diff:
```python
import functools

import jax
import jax.numpy as jnp
import numpy as np
from jax import lax
from jax.experimental import pallas as pl
from jax.experimental.pallas import tpu as pltpu
from jax.sharding import PartitionSpec as P

EPS = 1e-06
SIDE = 4
MOST = 6
BF16 = jnp.bfloat16
F32 = jnp.float32


def dot(a, b):
    return lax.dot_general(a, b, (((1,), (0,)), ((), ())), preferred_element_type=F32)


def dot_t(a, b):
    return lax.dot_general(a, b, (((1,), (1,)), ((), ())), preferred_element_type=F32)


def constants():
    per = SIDE * MOST
    r = np.arange(4 * per)
    half, chunk, plane, place = r // (2 * per), r // per % 2, r // MOST % SIDE, r % MOST
    slot_lane = (2 * plane + half) * MOST + place
    slots = np.zeros((2, 2, 4 * per, 128))
    for d in range(2):
        for c in range(2):
            slots[d, c, r, slot_lane + 64 * d] = chunk == c
    return jnp.asarray(slots, BF16)


def sixth(i):
    return (i * 683) >> 12


def one_hot(shape, place):
    row = lax.broadcasted_iota(jnp.int32, shape, 0)
    col = lax.broadcasted_iota(jnp.int32, shape, 1)
    return jnp.where(place(row, col), 1.0, 0.0).astype(BF16)


N_SEMS = 72


def kernel(
    acts, grads, saved_ref, gain_ref, gate_w, up_w, down_w, f_routes, f_gates, b_routes, b_gates,
    slot_of,
    out_ref, din_ref,
    in_buf, cot_buf, norm_buf, ysend, yrecv, zsend, zrecv, xbuf, w1, wd, part, psend, precv, act,
    dgu, mine, rsopp, rsrecv, rssend, rsin, zpack, zret, ypack, yret,
    pick, pick_t, swap,
    send_sem, recv_sem, copy_sem,
):
    tokens, width = saved_ref.shape[1], saved_ref.shape[2]
    half_d, chunk = width // 2, width // 4
    rows = xbuf.shape[1] * xbuf.shape[2]
    block = xbuf.shape[2]
    hb = block // 2
    hid = wd.shape[0] // 2
    packed_rows = SIDE * yrecv.shape[2]
    pipe = lax.axis_index("pipe")
    n_pipe = lax.axis_size("pipe")
    me = lax.axis_index("expert")
    z, y, x = me // (SIDE * SIDE), me // SIDE % SIDE, me % SIDE
    h, yl = y // 2, y % 2
    other = 1 - yl

    def at(zz, yy, xx):
        return (pipe, (zz * SIDE + yy) * SIDE + xx)

    ahead, behind = (lax.rem(pipe + 1, n_pipe), me), (lax.rem(pipe + n_pipe - 1, n_pipe), me)
    zs = [lax.rem(z + k, SIDE) for k in range(SIDE)]
    ys = [lax.rem(y + k, SIDE) for k in range(SIDE)]
    xr, xo, xl = (lax.rem(x + k, SIDE) for k in (1, 2, 3))
    right, left = at(z, y, xr), at(z, y, xl)
    mate = at(z, h * 2 + other, x)
    z_peers = [at(zs[k], y, x) for k in (1, 2, 3)]
    y_peers = [at(z, ys[k], x) for k in (1, 2, 3)]

    barrier = pltpu.get_barrier_semaphore()
    peers = [ahead, behind, right, left] + z_peers + y_peers
    for p in peers:
        pl.semaphore_signal(barrier, inc=1, device_id=p, device_id_type=pl.DeviceIdType.MESH)
    pl.semaphore_wait(barrier, len(peers))

    started = []

    def send(src, dst, to):
        i = len(started)
        c = pltpu.make_async_remote_copy(
            src_ref=src, dst_ref=dst, send_sem=send_sem.at[i], recv_sem=recv_sem.at[i],
            device_id=to, device_id_type=pl.DeviceIdType.MESH,
        )
        c.start()
        started.append(c)
        return c

    local = []

    def fetch(src, dst):
        c = pltpu.make_async_copy(src, dst, copy_sem.at[len(local)])
        c.start()
        local.append(c)
        return c

    F, B, C = 0, 1, 2

    c_acts = send(acts.at[0], in_buf, ahead)
    c_grads = send(grads.at[0], cot_buf, behind)

    eye = lax.broadcasted_iota(jnp.int32, (tokens, tokens), 0) == lax.broadcasted_iota(
        jnp.int32, (tokens, tokens), 1)
    before = lax.broadcasted_iota(jnp.int32, (tokens, tokens), 0) > lax.broadcasted_iota(
        jnp.int32, (tokens, tokens), 1)
    lane = lax.broadcasted_iota(jnp.int32, (tokens, 128), 1)
    is_f = lane < 64
    lane64 = lane & 63
    lane_expert = (lane64 * 43) >> 8
    lane_place = lane64 - lane_expert * MOST

    def column(ref, k):
        return jnp.sum(jnp.where(eye, ref[0, k:k + 1, :].astype(F32), 0.0), axis=1, keepdims=True)

    le = lane_expert.astype(F32)
    weight, named = 0.0, 0.0
    for k in range(2):
        hit = le == jnp.where(is_f, column(f_routes, k), column(b_routes, k))
        weight = weight + jnp.where(hit, jnp.where(is_f, column(f_gates, k), column(b_gates, k)), 0.0)
        named = named + jnp.where(hit, 1.0, 0.0)
    earlier = dot(jnp.where(before, 1.0, 0.0).astype(BF16), named.astype(BF16))
    table = jnp.where(earlier == lane_place.astype(F32), weight, 0.0)
    chosen = jnp.where(table > 0, 1.0, 0.0).astype(BF16)
    selects = [[dot_t(slot_of[d, c], chosen).astype(BF16) for c in range(2)] for d in range(2)]

    def scale_of(v):
        return lax.rsqrt(jnp.mean(v * v, axis=-1, keepdims=True) + EPS)

    gain = gain_ref[...]

    def y_spread(a, ref):
        s = selects[0 if a == F else 1]
        for k in range(2):
            got = None
            for c in range(2):
                col = k * half_d + c * chunk
                part_c = dot(s[c], ref[:, col:col + chunk])
                got = part_c if got is None else got + part_c
            got = got.astype(BF16)
            ysend[a, k, 0] = got[:yrecv.shape[2]]
            ysend[a, k, 1] = got[yrecv.shape[2]:]
        cs = [
            send(ysend.at[a, ys[k] % 2, ys[k] // 2], yrecv.at[a, y], y_peers[k - 1])
            for k in (1, 2, 3)
        ]
        yrecv[a, y] = ysend[a, yl, h]
        return cs

    def unpacked(i, c):
        return i + (sixth(i) >> 2) * per + c * per

    def swapped(i):
        i6 = sixth(i)
        two = i6 & 3
        return ((two * 2 + ((i6 >> 2) & 1)) * SIDE + (i6 >> 3)) * MOST + i - i6 * MOST

    def z_spread(a, cy):
        for c in cy:
            c.wait_recv()
        got = dot(swap[...], yrecv[a].reshape(packed_rows, chunk)).astype(BF16)
        zsend[a] = got.reshape(zsend.shape[1:])
        cs = [send(zsend.at[a, zs[k]], zrecv.at[a, z], z_peers[k - 1]) for k in (1, 2, 3)]
        zrecv[a, z] = zsend[a, z]
        return cs

    def x_spread(a, cz):
        for c in cz:
            c.wait_recv()
        packed = zrecv[a].reshape(packed_rows, chunk)
        for c in range(2):
            xbuf[a, x, :, c * chunk:(c + 1) * chunk] = dot(pick[c], packed).astype(BF16)
        return [send(xbuf.at[a, x], xbuf.at[a, x], right), send(xbuf.at[a, x], xbuf.at[a, x], left)]

    def x_forward(a, cx):
        cx[0].wait_recv()
        one = send(xbuf.at[a, xl, 0:hb], xbuf.at[a, xl, 0:hb], right)
        cx[1].wait_recv()
        two = send(xbuf.at[a, xr, hb:block], xbuf.at[a, xr, hb:block], left)
        return [one, two]

    def gathered(a, cf):
        for c in cf:
            c.wait_recv()
        return xbuf[a].reshape(rows, half_d)

    v = saved_ref[0].astype(F32)
    norm_buf[B] = (v * scale_of(v) * gain).astype(BF16)
    cy = {B: y_spread(B, norm_buf.at[B])}

    def d_half(k):
        return pl.ds(pl.multiple_of(k * half_d, half_d), half_d)

    def hidden(k):
        return pl.ds(pl.multiple_of(k * hid, hid), hid)

    per = block // SIDE
    swap[...] = one_hot(swap.shape, lambda i, j: j == swapped(i))
    for c in range(2):
        pick[c] = one_hot(pick.shape[1:], lambda i, j: j == unpacked(i, c))
        pick_t[c] = one_hot(pick_t.shape[1:], lambda i, j: i == unpacked(j, c))

    f_gu = [fetch(gate_w.at[0, d_half(yl), :], w1.at[yl, :, 0:hid]),
            fetch(up_w.at[0, d_half(yl), :], w1.at[yl, :, hid:2 * hid])]
    f_d = fetch(down_w.at[0, :, d_half(yl)], wd.at[hidden(yl), :])

    cz = {B: z_spread(B, cy[B])}
    c_acts.wait_recv()
    v = in_buf[...].astype(F32)
    norm_buf[F] = (v * scale_of(v) * gain).astype(BF16)
    cy[F] = y_spread(F, norm_buf.at[F])
    c_grads.wait_recv()
    cy[C] = y_spread(C, cot_buf)
    c_gu = [send(gate_w.at[0, d_half(other), :], w1.at[yl, :, 0:hid], mate),
            send(up_w.at[0, d_half(other), :], w1.at[yl, :, hid:2 * hid], mate)]
    c_d = send(down_w.at[0, :, d_half(other)], wd.at[hidden(yl), :], mate)
    cz[F] = z_spread(F, cy[F])
    cx = {B: x_spread(B, cz[B])}
    cz[C] = z_spread(C, cy[C])
    cf = {B: x_forward(B, cx[B])}
    cx[F] = x_spread(F, cz[F])
    cx[C] = x_spread(C, cz[C])
    cf[F] = x_forward(F, cx[F])

    for c in f_gu:
        c.wait()
    for c in c_gu:
        c.wait_recv()

    def gate_up(a):
        r = gathered(a, cf[a])
        psend[a] = dot(r, w1[other]).astype(BF16)
        c = send(psend.at[a], precv.at[a], mate)
        part[a] = dot(r, w1[yl])
        return c

    cp = {B: gate_up(B)}
    cp[F] = gate_up(F)
    cf[C] = x_forward(C, cx[C])

    cp[F].wait_recv()
    gu = part[F] + precv[F].astype(F32)
    gate, up = gu[:, :hid], gu[:, hid:]
    act[yl] = (gate * jax.nn.sigmoid(gate) * up).astype(BF16)
    c_act = send(act.at[yl], act.at[yl], mate)
    f_d.wait()
    c_d.wait_recv()

    def reduce_one(d, block_of):
        rsopp[d] = block_of(xo).astype(BF16)
        one = send(rsopp.at[d, 0:hb], rsrecv.at[d, 0], right)
        two = send(rsopp.at[d, hb:block], rsrecv.at[d, 1], left)
        mine[d, 0] = block_of(xr)
        mine[d, 1] = block_of(xl)
        mine[d, 2] = block_of(x)
        return [one, two]

    def reduce_two(d, cr):
        cr[0].wait_recv()
        rssend[d, 0, 0:hb] = (mine[d, 0, 0:hb] + rsrecv[d, 0].astype(F32)).astype(BF16)
        rssend[d, 0, hb:block] = mine[d, 0, hb:block].astype(BF16)
        one = send(rssend.at[d, 0], rsin.at[d, 0], right)
        cr[1].wait_recv()
        rssend[d, 1, hb:block] = (mine[d, 1, hb:block] + rsrecv[d, 1].astype(F32)).astype(BF16)
        rssend[d, 1, 0:hb] = mine[d, 1, 0:hb].astype(BF16)
        two = send(rssend.at[d, 1], rsin.at[d, 1], left)
        return [one, two]

    def z_return(d, cr):
        for c in cr:
            c.wait_recv()
        total = mine[d, 2] + rsin[d, 0].astype(F32) + rsin[d, 1].astype(F32)
        total = total.astype(BF16)
        packed = dot(pick_t[0], total[:, :chunk]) + dot(pick_t[1], total[:, chunk:])
        zpack[d] = packed.astype(BF16).reshape(zpack.shape[1:])
        cs = [send(zpack.at[d, zs[k]], zret.at[d, z], z_peers[k - 1]) for k in (1, 2, 3)]
        zret[d, z] = zpack[d, z]
        return cs

    def y_return(d, cr):
        for c in cr:
            c.wait_recv()
        got = dot(swap[...], zret[d].reshape(packed_rows, chunk)).astype(BF16)
        ypack[d] = got.reshape(ypack.shape[1:])
        cs = [send(ypack.at[d, ys[k]], yret.at[d, yl, h], y_peers[k - 1]) for k in (1, 2, 3)]
        yret[d, yl, h] = ypack[d, y]
        return cs

    w_hi = table.astype(BF16)
    w_lo = (table - w_hi.astype(F32)).astype(BF16)

    def combine(d, cr):
        hi = [dot_t(w_hi, slot_of[d, c]).astype(BF16) for c in range(2)]
        lo = [dot_t(w_lo, slot_of[d, c]).astype(BF16) for c in range(2)]
        for c in cr:
            c.wait_recv()
        parts = []
        for k in range(2):
            slots = yret[d, k].reshape(2 * yret.shape[3], chunk)
            for c in range(2):
                parts.append(dot(hi[c], slots) + dot(lo[c], slots))
        return jnp.concatenate(parts, axis=1)

    r = gathered(C, cf[C])
    psend[C, :, 0:hid] = dot_t(r, wd[hidden(other), :]).astype(BF16)
    cp[C] = send(psend.at[C, :, 0:hid], precv.at[C, :, 0:hid], mate)
    d_part = dot_t(r, wd[hidden(yl), :])

    c_act.wait_recv()

    def f_block(k):
        at_k = pl.ds(pl.multiple_of(k * block, block), block)
        return dot(act[0, at_k, :], wd[0:hid, :]) + dot(act[1, at_k, :], wd[hid:2 * hid, :])

    cr_f = reduce_one(0, f_block)

    cp[B].wait_recv()
    gu = part[B] + precv[B].astype(F32)
    gate, up = gu[:, :hid], gu[:, hid:]
    sigma = jax.nn.sigmoid(gate)
    by_gate = up * sigma * (1.0 + gate * (1.0 - sigma))
    by_up = gate * sigma
    cp[C].wait_recv()
    d_act = d_part + precv[C, :, 0:hid].astype(F32)
    dgu[yl, :, 0:hid] = (d_act * by_gate).astype(BF16)
    dgu[yl, :, hid:2 * hid] = (d_act * by_up).astype(BF16)
    c_dgu = send(dgu.at[yl], dgu.at[yl], mate)

    cr_f = reduce_two(0, cr_f)

    def b_block(k):
        at_k = pl.ds(pl.multiple_of(k * block, block), block)
        return dot_t(dgu[0, at_k, :], w1[0]) + dot_t(dgu[1, at_k, :], w1[1])

    c_dgu.wait_recv()
    cr_b = reduce_one(1, b_block)
    cr_f = z_return(0, cr_f)
    cr_b = reduce_two(1, cr_b)
    cr_f = y_return(0, cr_f)
    cr_b = z_return(1, cr_b)

    out_ref[0] = (in_buf[...].astype(F32) + combine(0, cr_f)).astype(BF16)

    cr_b = y_return(1, cr_b)
    v = saved_ref[0].astype(F32)
    scale = scale_of(v)
    dn = combine(1, cr_b) * gain
    d_in = scale * dn - v * (scale * scale * scale) * jnp.mean(dn * v, axis=-1, keepdims=True)
    din_ref[0] = (cot_buf[...].astype(F32) + d_in).astype(BF16)

    for c in started:
        c.wait_send()


def local(*args):
    held_acts = args[0]
    tokens, width = held_acts.shape[1:]
    hid = args[4].shape[2]
    per = SIDE * MOST
    block = SIDE * per
    rows = SIDE * block
    half_d, chunk = width // 2, width // 4
    args = args[:7] + tuple(jnp.swapaxes(a, 1, 2) for a in args[7:])
    vmem, hbm = pl.BlockSpec(memory_space=pltpu.VMEM), pl.BlockSpec(memory_space=pl.ANY)
    out = jax.ShapeDtypeStruct((1, tokens, width), BF16)
    V = pltpu.VMEM
    return pl.pallas_call(
        kernel,
        out_shape=(out, out),
        in_specs=[hbm, hbm, vmem, vmem, hbm, hbm, hbm] + [vmem] * 5,
        out_specs=(vmem, vmem),
        scratch_shapes=[
            V((tokens, width), BF16),
            V((tokens, width), BF16),
            V((2, tokens, width), BF16),
            V((3, 2, 2, 2 * per, chunk), BF16),
            V((3, SIDE, 2 * per, chunk), BF16),
            V((3, SIDE, 2 * per, chunk), BF16),
            V((3, SIDE, 2 * per, chunk), BF16),
            V((3, SIDE, block, half_d), BF16),
            V((2, half_d, 2 * hid), BF16),
            V((2 * hid, half_d), BF16),
            V((2, rows, 2 * hid), F32),
            V((3, rows, 2 * hid), BF16),
            V((3, rows, 2 * hid), BF16),
            V((2, rows, hid), BF16),
            V((2, rows, 2 * hid), BF16),
            V((2, 3, block, half_d), F32),
            V((2, block, half_d), BF16),
            V((2, 2, block // 2, half_d), BF16),
            V((2, 2, block, half_d), BF16),
            V((2, 2, block, half_d), BF16),
            V((2, SIDE, 2 * per, chunk), BF16),
            V((2, SIDE, 2 * per, chunk), BF16),
            V((2, SIDE, 2 * per, chunk), BF16),
            V((2, 2, 2, 2 * per, chunk), BF16),
            V((2, block, 2 * block), BF16),
            V((2, 2 * block, block), BF16),
            V((2 * block, 2 * block), BF16),
            pltpu.SemaphoreType.DMA((N_SEMS,)),
            pltpu.SemaphoreType.DMA((N_SEMS,)),
            pltpu.SemaphoreType.DMA((3,)),
        ],
        compiler_params=pltpu.CompilerParams(
            collective_id=0, has_side_effects=True, vmem_limit_bytes=58 * 1024 * 1024
        ),
    )(*args, constants())


def solution(mesh):
    return jax.shard_map(
        local,
        mesh=mesh,
        in_specs=(
            P("pipe", "expert", None),
            P("pipe", "expert", None),
            P("pipe", "expert", None),
            P("pipe", None),
            P("pipe", None, "expert"),
            P("pipe", None, "expert"),
            P("pipe", "expert", None),
            P("pipe", "expert", None),
            P("pipe", "expert", None),
            P("pipe", "expert", None),
            P("pipe", "expert", None),
        ),
        out_specs=(P("pipe", "expert", None), P("pipe", "expert", None)),
        check_vma=False,
    )
```

time: 139 us -> 117 us (0.84)
  the two profiles are of different devices: /device:TPU:18 before, /device:TPU:2 now
where the time goes in v2:
time: 117 us
  Pallas kernels  114 us (97%)
  local copies, waits for them, and re-layouts  2.24 us (2%)
    pallas_call x1, Pallas kernels, local(): pl.pallas_call(kernel, out_shape=(out, out), in_specs=[hbm, hbm, vmem, vm...  114 us

profile of v2, /device:TPU:2, one launch (start us, length us, event | category | flops | bytes accessed | tf_op | source)
XLA Modules:
  0.0 117.3 jit_solution(13412087906666416913)
XLA Ops:
  0.6 114.4 %shard_map.131 = (bf16[1,16,3584]{2,1,0:T(8,128)(2,1)}, bf16[1,16,3584]{2,1,0:T(8,128)(2,1)}) custom-call(bf16[1,16,3584]{2,1,0:T(8,128)(2,1)} %acts.1, bf16[1,16,3584]{2,1,0:T(8,128)(2,1)} %grads.1, bf16[1,16,3584]{2,1,0:T(8,128)(2,1)} %saved_ref.1, f32[1,3584]{1,0:T(1,128)} %gain_ref.1, bf16[1,3584,128]{2,1,0:T(8,128)(2,1)} %gate_w.1, ...), custom_call_target="tpu_custom_call" | custom-call | tf_op jit(solution)/shard_map/pallas_call | solution.py:381
  115.1 0.0 copy-start
  115.1 1.6 %copy.16 = bf16[1,16,3584]{2,1,0:T(8,128)(2,1)} copy(bf16[1,16,3584]{2,1,0:T(8,128)(2,1)} %get-tuple-element.4) | data formatting | bytes 229376
  116.7 0.0 copy-done
  116.7 0.6 copy.17
Async XLA Ops:
  115.1 1.6 %copy-start = (bf16[1,16,3584]{2,1,0:T(8,128)(2,1)S(1)}, bf16[1,16,3584]{2,1,0:T(8,128)(2,1)}, u32[]{:S(2)}) copy-start(bf16[1,16,3584]{2,1,0:T(8,128)(2,1)} %get-tuple-element.5) | copy-start | bytes 344068

commit v3 on v2

v3 whole, which is shorter than its diff:
```python
import functools

import jax
import jax.numpy as jnp
import numpy as np
from jax import lax
from jax.experimental import pallas as pl
from jax.experimental.pallas import tpu as pltpu
from jax.sharding import PartitionSpec as P

EPS = 1e-06
SIDE = 4
MOST = 6
BF16 = jnp.bfloat16
F32 = jnp.float32


def dot(a, b):
    return lax.dot_general(a, b, (((1,), (0,)), ((), ())), preferred_element_type=F32)


def dot_t(a, b):
    return lax.dot_general(a, b, (((1,), (1,)), ((), ())), preferred_element_type=F32)


def constants():
    per = SIDE * MOST
    r = np.arange(4 * per)
    half, chunk, plane, place = r // (2 * per), r // per % 2, r // MOST % SIDE, r % MOST
    slot_lane = (2 * plane + half) * MOST + place
    slots = np.zeros((2, 2, 4 * per, 128))
    for d in range(2):
        for c in range(2):
            slots[d, c, r, slot_lane + 64 * d] = chunk == c
    return jnp.asarray(slots, BF16)


def sixth(i):
    return (i * 683) >> 12


def one_hot(shape, place):
    row = lax.broadcasted_iota(jnp.int32, shape, 0)
    col = lax.broadcasted_iota(jnp.int32, shape, 1)
    return jnp.where(place(row, col), 1.0, 0.0).astype(BF16)


N_SEMS = 112


def kernel(
    acts, grads, saved_in, gain_in, gate_w, up_w, down_w, fr_in, fg_in, br_in, bg_in, slot_in,
    out_ref, din_ref,
    saved_ref, gain_ref, f_routes, f_gates, b_routes, b_gates, slot_of,
    in_buf, cot_buf, norm_buf, ysend, yrecv, zsend, xbuf, rbuf, w1, wd, part, psend, precv, act,
    dgu, mine, rsopp, rsrecv, rssend, rsin, zpack, zret, ypack, yret,
    pick, pick_t, swap,
    send_sem, recv_sem, copy_sem,
):
    tokens, width = saved_ref.shape[1], saved_ref.shape[2]
    half_d, chunk = width // 2, width // 4
    rows = rbuf.shape[1]
    block = rows // SIDE
    per = block // SIDE
    hid = wd.shape[0] // 2
    packed_rows = 2 * block
    pipe = lax.axis_index("pipe")
    n_pipe = lax.axis_size("pipe")
    me = lax.axis_index("expert")
    z, y, x = me // (SIDE * SIDE), me // SIDE % SIDE, me % SIDE
    h, yl = y // 2, y % 2
    other = 1 - yl

    def at(zz, yy, xx):
        return (pipe, (zz * SIDE + yy) * SIDE + xx)

    ahead, behind = (lax.rem(pipe + 1, n_pipe), me), (lax.rem(pipe + n_pipe - 1, n_pipe), me)
    zs = [lax.rem(z + k, SIDE) for k in range(SIDE)]
    zi = [lax.rem(z + SIDE - k, SIDE) for k in range(SIDE)]
    ys = [lax.rem(y + k, SIDE) for k in range(SIDE)]
    xr, xo, xl = (lax.rem(x + k, SIDE) for k in (1, 2, 3))
    right, left = at(z, y, xr), at(z, y, xl)
    mate = at(z, h * 2 + other, x)
    z_peers = [at(zs[k], y, x) for k in (1, 2, 3)]
    y_peers = [at(z, ys[k], x) for k in (1, 2, 3)]

    barrier = pltpu.get_barrier_semaphore()
    peers = [ahead, behind, right, left] + z_peers + y_peers
    for p in peers:
        pl.semaphore_signal(barrier, inc=1, device_id=p, device_id_type=pl.DeviceIdType.MESH)

    started = []

    def send(src, dst, to):
        i = len(started)
        c = pltpu.make_async_remote_copy(
            src_ref=src, dst_ref=dst, send_sem=send_sem.at[i], recv_sem=recv_sem.at[i],
            device_id=to, device_id_type=pl.DeviceIdType.MESH,
        )
        c.start()
        started.append(c)
        return c

    local = []

    def fetch(src, dst):
        c = pltpu.make_async_copy(src, dst, copy_sem.at[len(local)])
        c.start()
        local.append(c)
        return c

    F, B, C = 0, 1, 2

    inputs = [
        fetch(src, dst)
        for src, dst in (
            (fr_in, f_routes), (fg_in, f_gates), (br_in, b_routes), (bg_in, b_gates),
            (slot_in, slot_of), (saved_in, saved_ref), (gain_in, gain_ref),
        )
    ]
    for c in inputs:
        c.wait()

    eye = lax.broadcasted_iota(jnp.int32, (tokens, tokens), 0) == lax.broadcasted_iota(
        jnp.int32, (tokens, tokens), 1)
    before = lax.broadcasted_iota(jnp.int32, (tokens, tokens), 0) > lax.broadcasted_iota(
        jnp.int32, (tokens, tokens), 1)
    lane = lax.broadcasted_iota(jnp.int32, (tokens, 128), 1)
    is_f = lane < 64
    lane64 = lane & 63
    lane_expert = (lane64 * 43) >> 8
    lane_place = lane64 - lane_expert * MOST

    def column(ref, k):
        return jnp.sum(jnp.where(eye, ref[0, k:k + 1, :].astype(F32), 0.0), axis=1, keepdims=True)

    le = lane_expert.astype(F32)
    weight, named = 0.0, 0.0
    for k in range(2):
        hit = le == jnp.where(is_f, column(f_routes, k), column(b_routes, k))
        weight = weight + jnp.where(hit, jnp.where(is_f, column(f_gates, k), column(b_gates, k)), 0.0)
        named = named + jnp.where(hit, 1.0, 0.0)
    earlier = dot(jnp.where(before, 1.0, 0.0).astype(BF16), named.astype(BF16))
    table = jnp.where(earlier == lane_place.astype(F32), weight, 0.0)
    chosen = jnp.where(table > 0, 1.0, 0.0).astype(BF16)
    selects = [[dot_t(slot_of[d, c], chosen).astype(BF16) for c in range(2)] for d in range(2)]

    def scale_of(v):
        return lax.rsqrt(jnp.mean(v * v, axis=-1, keepdims=True) + EPS)

    gain = gain_ref[...]

    def y_pack(a, ref):
        s = selects[0 if a == F else 1]
        for k in range(2):
            got = None
            for c in range(2):
                col = k * half_d + c * chunk
                part_c = dot(s[c], ref[:, col:col + chunk])
                got = part_c if got is None else got + part_c
            got = got.astype(BF16)
            ysend[a, k, 0] = got[:2 * per]
            ysend[a, k, 1] = got[2 * per:]

    def y_spread(a):
        cs = [
            send(ysend.at[a, ys[k] % 2, ys[k] // 2], yrecv.at[a, y], y_peers[k - 1])
            for k in (1, 2, 3)
        ]
        yrecv[a, y] = ysend[a, yl, h]
        return cs

    def unpacked(i, c):
        return i + (sixth(i) >> 2) * per + c * per

    def swapped(i):
        i6 = sixth(i)
        two = i6 & 3
        return ((two * 2 + ((i6 >> 2) & 1)) * SIDE + (i6 >> 3)) * MOST + i - i6 * MOST

    def z_spread(a, cy):
        for c in cy:
            c.wait_recv()
        got = dot(swap[...], yrecv[a].reshape(packed_rows, chunk)).astype(BF16)
        zsend[a] = got.reshape(zsend.shape[1:])
        cs = [send(zsend.at[a, zs[k]], xbuf.at[a, x, z], z_peers[k - 1]) for k in (1, 2, 3)]
        xbuf[a, x, z] = zsend[a, z]
        return [None] + cs

    xs = [[None] * SIDE for _ in range(3)]
    xf = [[], [], []]

    def x_send(a, i, cz):
        if i > 0:
            cz[i].wait_recv()
        ref = xbuf.at[a, x, zi[i]]
        xs[a][i] = (send(ref, ref, right), send(ref, ref, left))

    def x_forward(a, i):
        xs[a][i][i % 2].wait_recv()
        ref = xbuf.at[a, (xl, xr)[i % 2], zi[i]]
        xf[a].append(send(ref, ref, (right, left)[i % 2]))

    def gathered(a):
        for i in range(SIDE):
            xs[a][i][1 - i % 2].wait_recv()
        for c in xf[a]:
            c.wait_recv()
        for s in range(SIDE):
            packed = xbuf[a, s].reshape(packed_rows, chunk)
            for c in range(2):
                rbuf[a, s * block:(s + 1) * block, c * chunk:(c + 1) * chunk] = dot(
                    pick[c], packed).astype(BF16)
        return rbuf[a]

    v = saved_ref[0].astype(F32)
    norm_buf[B] = (v * scale_of(v) * gain).astype(BF16)
    y_pack(B, norm_buf.at[B])

    pl.semaphore_wait(barrier, len(peers))

    cy = {B: y_spread(B)}

    c_acts = send(acts.at[0], in_buf, ahead)
    c_grads = send(grads.at[0], cot_buf, behind)

    def d_half(k):
        return pl.ds(pl.multiple_of(k * half_d, half_d), half_d)

    def hidden(k):
        return pl.ds(pl.multiple_of(k * hid, hid), hid)

    def weight_rows(ref, lane0, k):
        rows_k = pl.ds(pl.multiple_of(other * half_d + k * chunk, chunk), chunk)
        dst = w1.at[yl, k * chunk:(k + 1) * chunk, lane0:lane0 + hid]
        return send(ref.at[0, rows_k, :], dst, mate)

    c_gu = [weight_rows(gate_w, 0, 0)]
    f_gu = [fetch(gate_w.at[0, d_half(yl), :], w1.at[yl, :, 0:hid]),
            fetch(up_w.at[0, d_half(yl), :], w1.at[yl, :, hid:2 * hid])]
    f_d = fetch(down_w.at[0, :, d_half(yl)], wd.at[hidden(yl), :])

    swap[...] = one_hot(swap.shape, lambda i, j: j == swapped(i))
    for c in range(2):
        pick[c] = one_hot(pick.shape[1:], lambda i, j: j == unpacked(i, c))
        pick_t[c] = one_hot(pick_t.shape[1:], lambda i, j: i == unpacked(j, c))

    cz = {B: z_spread(B, cy[B])}
    x_send(B, 0, cz[B])
    c_acts.wait_recv()
    v = in_buf[...].astype(F32)
    norm_buf[F] = (v * scale_of(v) * gain).astype(BF16)
    y_pack(F, norm_buf.at[F])
    cy[F] = y_spread(F)
    c_grads.wait_recv()
    y_pack(C, cot_buf)
    cy[C] = y_spread(C)
    c_gu += [weight_rows(gate_w, 0, 1), weight_rows(up_w, hid, 0), weight_rows(up_w, hid, 1)]
    c_d = send(down_w.at[0, :, d_half(other)], wd.at[hidden(yl), :], mate)
    for i in (1, 2, 3):
        x_send(B, i, cz[B])
    x_forward(B, 0)
    cz[F] = z_spread(F, cy[F])
    x_send(F, 0, cz[F])
    x_forward(B, 1)
    cz[C] = z_spread(C, cy[C])
    x_forward(B, 2)
    x_forward(B, 3)
    for i in (1, 2, 3):
        x_send(F, i, cz[F])
    x_send(C, 0, cz[C])
    for i in range(SIDE):
        x_forward(F, i)
    for i in (1, 2, 3):
        x_send(C, i, cz[C])

    def gate_up(a):
        r = gathered(a)
        psend[a] = dot(r, w1[other]).astype(BF16)
        c = send(psend.at[a], precv.at[a], mate)
        part[a] = dot(r, w1[yl])
        return c

    for c in f_gu:
        c.wait()
    for c in c_gu:
        c.wait_recv()
    cp = {F: gate_up(F)}
    for i in range(SIDE):
        x_forward(C, i)
    cp[B] = gate_up(B)

    cp[F].wait_recv()
    gu = part[F] + precv[F].astype(F32)
    gate, up = gu[:, :hid], gu[:, hid:]
    act[yl] = (gate * jax.nn.sigmoid(gate) * up).astype(BF16)
    c_act = send(act.at[yl], act.at[yl], mate)

    to_right, to_left = (2, 1), (3, 0)

    def reduce_start(d, block_of):
        rsopp[d] = block_of(xo).astype(BF16).reshape(rsopp.shape[1:])
        opp, got = {}, ({}, {})
        for i, j in zip(to_right, to_left):
            opp[i] = send(rsopp.at[d, zi[i]], rsrecv.at[d, zi[i]], right)
            opp[j] = send(rsopp.at[d, zi[j]], rsrecv.at[d, zi[j]], left)
        for n, (k, to, now) in enumerate(((xr, right, to_left), (xl, left, to_right))):
            mine[d, n] = block_of(k).reshape(mine.shape[2:])
            for i in now:
                rssend[d, n, zi[i]] = mine[d, n, zi[i]].astype(BF16)
                got[n][i] = send(rssend.at[d, n, zi[i]], rsin.at[d, n, zi[i]], to)
        mine[d, 2] = block_of(x).reshape(mine.shape[2:])
        return opp, got

    def reduce_finish(d, cr):
        opp, got = cr
        for pair in zip(to_right, to_left):
            for n, (i, to) in enumerate(zip(pair, (right, left))):
                opp[i].wait_recv()
                total = mine[d, n, zi[i]] + rsrecv[d, zi[i]].astype(F32)
                rssend[d, n, zi[i]] = total.astype(BF16)
                got[n][i] = send(rssend.at[d, n, zi[i]], rsin.at[d, n, zi[i]], to)
        return got

    def z_return(d, got):
        cs = []
        for i in (2, 3, 1, 0):
            got[0][i].wait_recv()
            got[1][i].wait_recv()
            total = mine[d, 2, zi[i]] + rsin[d, 0, zi[i]].astype(F32) + rsin[d, 1, zi[i]].astype(F32)
            if i == 0:
                zret[d, z] = total.astype(BF16)
            else:
                zpack[d, zi[i]] = total.astype(BF16)
                cs.append(send(zpack.at[d, zi[i]], zret.at[d, z], at(zi[i], y, x)))
        return cs

    def y_return(d, cr):
        for c in cr:
            c.wait_recv()
        got = dot(swap[...], zret[d].reshape(packed_rows, chunk)).astype(BF16)
        ypack[d] = got.reshape(ypack.shape[1:])
        cs = [send(ypack.at[d, ys[k]], yret.at[d, yl, h], y_peers[k - 1]) for k in (1, 2, 3)]
        yret[d, yl, h] = ypack[d, y]
        return cs

    w_hi = table.astype(BF16)
    w_lo = (table - w_hi.astype(F32)).astype(BF16)

    def combine(d, cr):
        hi = [dot_t(w_hi, slot_of[d, c]).astype(BF16) for c in range(2)]
        lo = [dot_t(w_lo, slot_of[d, c]).astype(BF16) for c in range(2)]
        for c in cr:
            c.wait_recv()
        parts = []
        for k in range(2):
            slots = yret[d, k].reshape(packed_rows // 2, chunk)
            for c in range(2):
                parts.append(dot(hi[c], slots) + dot(lo[c], slots))
        return jnp.concatenate(parts, axis=1)

    r = gathered(C)
    f_d.wait()
    c_d.wait_recv()
    psend[C, :, 0:hid] = dot_t(r, wd[hidden(other), :]).astype(BF16)
    cp[C] = send(psend.at[C, :, 0:hid], precv.at[C, :, 0:hid], mate)
    d_part = dot_t(r, wd[hidden(yl), :])

    c_act.wait_recv()

    def f_block(k):
        at_k = pl.ds(pl.multiple_of(k * block, block), block)
        a = jnp.concatenate([act[0, at_k, :], act[1, at_k, :]], axis=1)
        total = 0.0
        for c in range(2):
            total = total + dot(dot(pick_t[c], a).astype(BF16), wd[:, c * chunk:(c + 1) * chunk])
        return total

    cr_f = reduce_start(0, f_block)

    cp[B].wait_recv()
    gu = part[B] + precv[B].astype(F32)
    gate, up = gu[:, :hid], gu[:, hid:]
    sigma = jax.nn.sigmoid(gate)
    by_gate = up * sigma * (1.0 + gate * (1.0 - sigma))
    by_up = gate * sigma
    cp[C].wait_recv()
    d_act = d_part + precv[C, :, 0:hid].astype(F32)
    dgu[yl, :, 0:hid] = (d_act * by_gate).astype(BF16)
    dgu[yl, :, hid:2 * hid] = (d_act * by_up).astype(BF16)
    c_dgu = send(dgu.at[yl], dgu.at[yl], mate)

    cr_f = reduce_finish(0, cr_f)

    def b_block(k):
        at_k = pl.ds(pl.multiple_of(k * block, block), block)
        total = 0.0
        for s in range(2):
            for c in range(2):
                a = dot(pick_t[c], dgu[s, at_k, :]).astype(BF16)
                total = total + dot_t(a, w1[s, c * chunk:(c + 1) * chunk, :])
        return total

    c_dgu.wait_recv()
    cr_b = reduce_start(1, b_block)
    cr_f = z_return(0, cr_f)
    cr_b = reduce_finish(1, cr_b)
    cr_f = y_return(0, cr_f)
    cr_b = z_return(1, cr_b)

    out_ref[0] = (in_buf[...].astype(F32) + combine(0, cr_f)).astype(BF16)

    cr_b = y_return(1, cr_b)
    v = saved_ref[0].astype(F32)
    scale = scale_of(v)
    dn = combine(1, cr_b) * gain
    d_in = scale * dn - v * (scale * scale * scale) * jnp.mean(dn * v, axis=-1, keepdims=True)
    din_ref[0] = (cot_buf[...].astype(F32) + d_in).astype(BF16)

    for c in started:
        c.wait_send()


def local(*args):
    held_acts = args[0]
    tokens, width = held_acts.shape[1:]
    hid = args[4].shape[2]
    per = SIDE * MOST
    block = SIDE * per
    rows = SIDE * block
    half_d, chunk = width // 2, width // 4
    args = args[:7] + tuple(jnp.swapaxes(a, 1, 2) for a in args[7:])
    vmem, hbm = pl.BlockSpec(memory_space=pltpu.VMEM), pl.BlockSpec(memory_space=pl.ANY)
    out = jax.ShapeDtypeStruct((1, tokens, width), BF16)
    slots = constants()
    V = pltpu.VMEM
    packed = (SIDE, 2 * per, chunk)
    return pl.pallas_call(
        kernel,
        out_shape=(out, out),
        in_specs=[hbm] * 12,
        out_specs=(vmem, vmem),
        scratch_shapes=[
            V(args[2].shape, BF16),
            V(args[3].shape, F32),
            V(args[7].shape, jnp.int32),
            V(args[8].shape, F32),
            V(args[9].shape, jnp.int32),
            V(args[10].shape, F32),
            V(slots.shape, BF16),
            V((tokens, width), BF16),
            V((tokens, width), BF16),
            V((2, tokens, width), BF16),
            V((3, 2, 2) + packed[1:], BF16),
            V((3,) + packed, BF16),
            V((3,) + packed, BF16),
            V((3, SIDE) + packed, BF16),
            V((3, rows, half_d), BF16),
            V((2, half_d, 2 * hid), BF16),
            V((2 * hid, half_d), BF16),
            V((2, rows, 2 * hid), F32),
            V((3, rows, 2 * hid), BF16),
            V((3, rows, 2 * hid), BF16),
            V((2, rows, hid), BF16),
            V((2, rows, 2 * hid), BF16),
            V((2, 3) + packed, F32),
            V((2,) + packed, BF16),
            V((2,) + packed, BF16),
            V((2, 2) + packed, BF16),
            V((2, 2) + packed, BF16),
            V((2,) + packed, BF16),
            V((2,) + packed, BF16),
            V((2,) + packed, BF16),
            V((2, 2, 2) + packed[1:], BF16),
            V((2, block, 2 * block), BF16),
            V((2, 2 * block, block), BF16),
            V((2 * block, 2 * block), BF16),
            pltpu.SemaphoreType.DMA((N_SEMS,)),
            pltpu.SemaphoreType.DMA((N_SEMS,)),
            pltpu.SemaphoreType.DMA((10,)),
        ],
        compiler_params=pltpu.CompilerParams(
            collective_id=0, has_side_effects=True, vmem_limit_bytes=58 * 1024 * 1024
        ),
    )(*args, slots)


def solution(mesh):
    return jax.shard_map(
        local,
        mesh=mesh,
        in_specs=(
            P("pipe", "expert", None),
            P("pipe", "expert", None),
            P("pipe", "expert", None),
            P("pipe", None),
            P("pipe", None, "expert"),
            P("pipe", None, "expert"),
            P("pipe", "expert", None),
            P("pipe", "expert", None),
            P("pipe", "expert", None),
            P("pipe", "expert", None),
            P("pipe", "expert", None),
        ),
        out_specs=(P("pipe", "expert", None), P("pipe", "expert", None)),
        check_vma=False,
    )
```

time: 117 us -> 106 us (0.906)
  Pallas kernels: 114 us -> 103 us
    pallas_call x1, Pallas kernels: 114 us -> 103 us  [local(): pl.pallas_call(kernel, out_shape=(out, out), in_specs=[hbm] * 12, out_spe...]
where the time goes in v3:
time: 106 us
  Pallas kernels  103 us (97%)
  local copies, waits for them, and re-layouts  2.24 us (2%)
    pallas_call x1, Pallas kernels, local(): pl.pallas_call(kernel, out_shape=(out, out), in_specs=[hbm] * 12, out_spe...  103 us
    unnamed x4, local copies, waits for them, and re-layouts  2.24 us

profile of v3, /device:TPU:2, one launch (start us, length us, event | category | flops | bytes accessed | tf_op | source)
XLA Modules:
  0.0 106.0 jit_solution(13746806900291019333)
XLA Ops:
  0.6 103.1 %shard_map.131 = (bf16[1,16,3584]{2,1,0:T(8,128)(2,1)}, bf16[1,16,3584]{2,1,0:T(8,128)(2,1)}) custom-call(bf16[1,16,3584]{2,1,0:T(8,128)(2,1)} %acts.1, bf16[1,16,3584]{2,1,0:T(8,128)(2,1)} %grads.1, bf16[1,16,3584]{2,1,0:T(8,128)(2,1)} %saved_in.1, f32[1,3584]{1,0:T(1,128)} %gain_in.1, bf16[1,3584,128]{2,1,0:T(8,128)(2,1)} %gate_w.1, ...), custom_call_target="tpu_custom_call" | custom-call | tf_op jit(solution)/shard_map/pallas_call | solution.py:438
  103.8 0.0 copy-start
  103.8 1.6 %copy.16 = bf16[1,16,3584]{2,1,0:T(8,128)(2,1)} copy(bf16[1,16,3584]{2,1,0:T(8,128)(2,1)} %get-tuple-element.4) | data formatting | bytes 229376
  105.4 0.0 copy-done
  105.4 0.6 copy.17
Async XLA Ops:
  103.8 1.6 %copy-start = (bf16[1,16,3584]{2,1,0:T(8,128)(2,1)S(1)}, bf16[1,16,3584]{2,1,0:T(8,128)(2,1)}, u32[]{:S(2)}) copy-start(bf16[1,16,3584]{2,1,0:T(8,128)(2,1)} %get-tuple-element.5) | copy-start | bytes 344068

commit v4 on v3

--- a/solution.py
+++ b/solution.py
@@ -25,13 +25,12 @@
 
 def constants():
     per = SIDE * MOST
-    r = np.arange(4 * per)
-    half, chunk, plane, place = r // (2 * per), r // per % 2, r // MOST % SIDE, r % MOST
-    slot_lane = (2 * plane + half) * MOST + place
-    slots = np.zeros((2, 2, 4 * per, 128))
-    for d in range(2):
-        for c in range(2):
-            slots[d, c, r, slot_lane + 64 * d] = chunk == c
+    r = np.arange(2 * SIDE * per)
+    plane, place = r // (2 * per), r % MOST
+    slots = np.zeros((2, 2, len(r), 128))
+    for h in range(2):
+        for d in range(2):
+            slots[h, d, r, (2 * plane + h) * MOST + place + 64 * d] = 1
     return jnp.asarray(slots, BF16)
 
 
@@ -45,16 +44,16 @@
     return jnp.where(place(row, col), 1.0, 0.0).astype(BF16)
 
 
-N_SEMS = 112
+N_SEMS = 128
 
 
 def kernel(
     acts, grads, saved_in, gain_in, gate_w, up_w, down_w, fr_in, fg_in, br_in, bg_in, slot_in,
     out_ref, din_ref,
     saved_ref, gain_ref, f_routes, f_gates, b_routes, b_gates, slot_of,
-    in_buf, cot_buf, norm_buf, ysend, yrecv, zsend, xbuf, rbuf, w1, wd, part, psend, precv, act,
-    dgu, mine, rsopp, rsrecv, rssend, rsin, zpack, zret, ypack, yret,
-    pick, pick_t, swap,
+    in_buf, cot_buf, norm_buf, tab, ytok, zsend, xbuf, rbuf, w1, wd, part, d_part, psend, precv,
+    psend_c, precv_c, act, dgu, mine, rsopp, rsrecv, rssend, rsin, zpack, zret, ypack, yret,
+    pick, pick_t,
     send_sem, recv_sem, copy_sem,
 ):
     tokens, width = saved_ref.shape[1], saved_ref.shape[2]
@@ -75,13 +74,12 @@
         return (pipe, (zz * SIDE + yy) * SIDE + xx)
 
     ahead, behind = (lax.rem(pipe + 1, n_pipe), me), (lax.rem(pipe + n_pipe - 1, n_pipe), me)
-    zs = [lax.rem(z + k, SIDE) for k in range(SIDE)]
-    zi = [lax.rem(z + SIDE - k, SIDE) for k in range(SIDE)]
-    ys = [lax.rem(y + k, SIDE) for k in range(SIDE)]
+    zi = [z, z + 1 - 2 * (z % 2), lax.rem(z + 2, SIDE), SIDE - 1 - z]
+    ys = [y, y + 1 - 2 * (y % 2), SIDE - 1 - y, lax.rem(y + 2, SIDE)]
     xr, xo, xl = (lax.rem(x + k, SIDE) for k in (1, 2, 3))
     right, left = at(z, y, xr), at(z, y, xl)
     mate = at(z, h * 2 + other, x)
-    z_peers = [at(zs[k], y, x) for k in (1, 2, 3)]
+    z_peers = [at(zi[k], y, x) for k in (1, 2, 3)]
     y_peers = [at(z, ys[k], x) for k in (1, 2, 3)]
 
     barrier = pltpu.get_barrier_semaphore()
@@ -115,7 +113,7 @@
         fetch(src, dst)
         for src, dst in (
             (fr_in, f_routes), (fg_in, f_gates), (br_in, b_routes), (bg_in, b_gates),
-            (slot_in, slot_of), (saved_in, saved_ref), (gain_in, gain_ref),
+            (slot_in.at[h], slot_of), (saved_in, saved_ref), (gain_in, gain_ref),
         )
     ]
     for c in inputs:
@@ -141,49 +139,35 @@
         weight = weight + jnp.where(hit, jnp.where(is_f, column(f_gates, k), column(b_gates, k)), 0.0)
         named = named + jnp.where(hit, 1.0, 0.0)
     earlier = dot(jnp.where(before, 1.0, 0.0).astype(BF16), named.astype(BF16))
-    table = jnp.where(earlier == lane_place.astype(F32), weight, 0.0)
-    chosen = jnp.where(table > 0, 1.0, 0.0).astype(BF16)
-    selects = [[dot_t(slot_of[d, c], chosen).astype(BF16) for c in range(2)] for d in range(2)]
+    tab[y] = jnp.where(earlier == lane_place.astype(F32), weight, 0.0)
 
     def scale_of(v):
         return lax.rsqrt(jnp.mean(v * v, axis=-1, keepdims=True) + EPS)
 
     gain = gain_ref[...]
 
-    def y_pack(a, ref):
-        s = selects[0 if a == F else 1]
-        for k in range(2):
-            got = None
-            for c in range(2):
-                col = k * half_d + c * chunk
-                part_c = dot(s[c], ref[:, col:col + chunk])
-                got = part_c if got is None else got + part_c
-            got = got.astype(BF16)
-            ysend[a, k, 0] = got[:2 * per]
-            ysend[a, k, 1] = got[2 * per:]
-
-    def y_spread(a):
+    def d_half(k):
+        return pl.ds(pl.multiple_of(k * half_d, half_d), half_d)
+
+    def y_spread(a, ref):
         cs = [
-            send(ysend.at[a, ys[k] % 2, ys[k] // 2], yrecv.at[a, y], y_peers[k - 1])
-            for k in (1, 2, 3)
+            send(ref.at[:, d_half(ys[k] % 2)], ytok.at[a, y], y_peers[k - 1]) for k in (1, 2, 3)
         ]
-        yrecv[a, y] = ysend[a, yl, h]
+        ytok[a, y] = ref[:, d_half(yl)]
         return cs
 
     def unpacked(i, c):
         return i + (sixth(i) >> 2) * per + c * per
-
-    def swapped(i):
-        i6 = sixth(i)
-        two = i6 & 3
-        return ((two * 2 + ((i6 >> 2) & 1)) * SIDE + (i6 >> 3)) * MOST + i - i6 * MOST
 
     def z_spread(a, cy):
         for c in cy:
             c.wait_recv()
-        got = dot(swap[...], yrecv[a].reshape(packed_rows, chunk)).astype(BF16)
-        zsend[a] = got.reshape(zsend.shape[1:])
-        cs = [send(zsend.at[a, zs[k]], xbuf.at[a, x, z], z_peers[k - 1]) for k in (1, 2, 3)]
+        got = 0.0
+        for c in range(2):
+            toks = ytok[a, :, :, c * chunk:(c + 1) * chunk].reshape(SIDE * tokens, chunk)
+            got = got + dot(selects[0 if a == F else 1][c], toks)
+        zsend[a] = got.astype(BF16).reshape(zsend.shape[1:])
+        cs = [send(zsend.at[a, zi[k]], xbuf.at[a, x, z], z_peers[k - 1]) for k in (1, 2, 3)]
         xbuf[a, x, z] = zsend[a, z]
         return [None] + cs
 
@@ -211,21 +195,15 @@
             for c in range(2):
                 rbuf[a, s * block:(s + 1) * block, c * chunk:(c + 1) * chunk] = dot(
                     pick[c], packed).astype(BF16)
-        return rbuf[a]
 
     v = saved_ref[0].astype(F32)
     norm_buf[B] = (v * scale_of(v) * gain).astype(BF16)
-    y_pack(B, norm_buf.at[B])
-
     pl.semaphore_wait(barrier, len(peers))
-
-    cy = {B: y_spread(B)}
 
     c_acts = send(acts.at[0], in_buf, ahead)
     c_grads = send(grads.at[0], cot_buf, behind)
-
-    def d_half(k):
-        return pl.ds(pl.multiple_of(k * half_d, half_d), half_d)
+    c_tab = [send(tab.at[y], tab.at[y], p) for p in y_peers]
+    cy = {B: y_spread(B, norm_buf.at[B])}
 
     def hidden(k):
         return pl.ds(pl.multiple_of(k * hid, hid), hid)
@@ -236,79 +214,121 @@
         return send(ref.at[0, rows_k, :], dst, mate)
 
     c_gu = [weight_rows(gate_w, 0, 0)]
+    def down_piece(q):
+        n = hid // SIDE
+        rows_q = pl.ds(pl.multiple_of(yl * hid + q * n, n), n)
+        return send(down_w.at[0, q * n:(q + 1) * n, d_half(other)], wd.at[rows_q, :], mate)
+
     f_gu = [fetch(gate_w.at[0, d_half(yl), :], w1.at[yl, :, 0:hid]),
             fetch(up_w.at[0, d_half(yl), :], w1.at[yl, :, hid:2 * hid])]
     f_d = fetch(down_w.at[0, :, d_half(yl)], wd.at[hidden(yl), :])
 
-    swap[...] = one_hot(swap.shape, lambda i, j: j == swapped(i))
     for c in range(2):
         pick[c] = one_hot(pick.shape[1:], lambda i, j: j == unpacked(i, c))
         pick_t[c] = one_hot(pick_t.shape[1:], lambda i, j: i == unpacked(j, c))
+
+    for c in c_tab:
+        c.wait_recv()
+    table = tab[...].reshape(SIDE * tokens, 128)
+    chosen = jnp.where(table > 0, 1.0, 0.0).astype(BF16)
+    w_hi = table.astype(BF16)
+    w_lo = (table - w_hi.astype(F32)).astype(BF16)
+
+    def matches(shape, dim, c):
+        row = lax.broadcasted_iota(jnp.int32, shape, dim)
+        token = lax.broadcasted_iota(jnp.int32, shape, 1 - dim)
+        return ((sixth(row) >> 2) & 1 == c) & (sixth(row) & 3 == token // tokens)
+
+    to_rows, to_tokens = (packed_rows, SIDE * tokens), (SIDE * tokens, packed_rows)
+    selects = [
+        [jnp.where(matches(to_rows, 0, c), dot_t(slot_of[d], chosen), 0.0).astype(BF16) for c in range(2)]
+        for d in range(2)
+    ]
 
     cz = {B: z_spread(B, cy[B])}
     x_send(B, 0, cz[B])
     c_acts.wait_recv()
     v = in_buf[...].astype(F32)
     norm_buf[F] = (v * scale_of(v) * gain).astype(BF16)
-    y_pack(F, norm_buf.at[F])
-    cy[F] = y_spread(F)
+    cy[F] = y_spread(F, norm_buf.at[F])
     c_grads.wait_recv()
-    y_pack(C, cot_buf)
-    cy[C] = y_spread(C)
+    cy[C] = y_spread(C, cot_buf)
     c_gu += [weight_rows(gate_w, 0, 1), weight_rows(up_w, hid, 0), weight_rows(up_w, hid, 1)]
-    c_d = send(down_w.at[0, :, d_half(other)], wd.at[hidden(yl), :], mate)
-    for i in (1, 2, 3):
-        x_send(B, i, cz[B])
+    c_d = [down_piece(q) for q in (0, 1)]
+    x_send(B, 1, cz[B])
     x_forward(B, 0)
+    x_send(B, 2, cz[B])
     cz[F] = z_spread(F, cy[F])
     x_send(F, 0, cz[F])
     x_forward(B, 1)
+    x_send(B, 3, cz[B])
     cz[C] = z_spread(C, cy[C])
+    x_send(C, 0, cz[C])
     x_forward(B, 2)
+    x_send(F, 1, cz[F])
     x_forward(B, 3)
-    for i in (1, 2, 3):
-        x_send(F, i, cz[F])
-    x_send(C, 0, cz[C])
-    for i in range(SIDE):
-        x_forward(F, i)
-    for i in (1, 2, 3):
-        x_send(C, i, cz[C])
-
-    def gate_up(a):
-        r = gathered(a)
-        psend[a] = dot(r, w1[other]).astype(BF16)
-        c = send(psend.at[a], precv.at[a], mate)
-        part[a] = dot(r, w1[yl])
-        return c
-
+    x_forward(F, 0)
+    x_send(F, 2, cz[F])
+    x_forward(F, 1)
+    x_send(F, 3, cz[F])
+    x_forward(C, 0)
+    x_forward(F, 2)
+    x_send(C, 1, cz[C])
+    x_forward(F, 3)
+    x_send(C, 2, cz[C])
+    x_forward(C, 1)
+    x_send(C, 3, cz[C])
+    gathered(B)
+
+    order = (xo, xr, xl, x)
+
+    def pair(src, dst):
+        return [send(src.at[k], dst.at[k], mate) for k in order]
+
+    def in_blocks(v):
+        return v.reshape(SIDE, block, v.shape[1])
+
+    gathered(F)
     for c in f_gu:
         c.wait()
     for c in c_gu:
         c.wait_recv()
-    cp = {F: gate_up(F)}
-    for i in range(SIDE):
-        x_forward(C, i)
-    cp[B] = gate_up(B)
-
-    cp[F].wait_recv()
-    gu = part[F] + precv[F].astype(F32)
-    gate, up = gu[:, :hid], gu[:, hid:]
-    act[yl] = (gate * jax.nn.sigmoid(gate) * up).astype(BF16)
-    c_act = send(act.at[yl], act.at[yl], mate)
+    cp = {}
+    psend[F] = in_blocks(dot(rbuf[F], w1[other])).astype(BF16)
+    cp[F] = pair(psend.at[F], precv.at[F])
+    c_d += [down_piece(q) for q in (2, 3)]
+    part[F] = in_blocks(dot(rbuf[F], w1[yl]))
+    x_forward(C, 2)
+
+    c_act = []
+    for n, k in enumerate(order):
+        cp[F][n].wait_recv()
+        gu = part[F, k] + precv[F, k].astype(F32)
+        gate, up = gu[:, :hid], gu[:, hid:]
+        act[yl, k] = (gate * jax.nn.sigmoid(gate) * up).astype(BF16)
+        c_act.append(send(act.at[yl, k], act.at[yl, k], mate))
+        if n == 0:
+            x_forward(C, 3)
+
+    psend[B] = in_blocks(dot(rbuf[B], w1[other])).astype(BF16)
+    part[B] = in_blocks(dot(rbuf[B], w1[yl]))
 
     to_right, to_left = (2, 1), (3, 0)
 
-    def reduce_start(d, block_of):
+    def reduce_start(d, block_of, ready):
+        ready[0].wait_recv()
         rsopp[d] = block_of(xo).astype(BF16).reshape(rsopp.shape[1:])
         opp, got = {}, ({}, {})
         for i, j in zip(to_right, to_left):
             opp[i] = send(rsopp.at[d, zi[i]], rsrecv.at[d, zi[i]], right)
             opp[j] = send(rsopp.at[d, zi[j]], rsrecv.at[d, zi[j]], left)
         for n, (k, to, now) in enumerate(((xr, right, to_left), (xl, left, to_right))):
+            ready[n + 1].wait_recv()
             mine[d, n] = block_of(k).reshape(mine.shape[2:])
             for i in now:
                 rssend[d, n, zi[i]] = mine[d, n, zi[i]].astype(BF16)
                 got[n][i] = send(rssend.at[d, n, zi[i]], rsin.at[d, n, zi[i]], to)
+        ready[3].wait_recv()
         mine[d, 2] = block_of(x).reshape(mine.shape[2:])
         return opp, got
 
@@ -336,73 +356,65 @@
         return cs
 
     def y_return(d, cr):
+        weighs = [
+            [jnp.where(matches(to_tokens, 1, c), dot_t(w, slot_of[d]), 0.0).astype(BF16) for w in (w_hi, w_lo)]
+            for c in range(2)
+        ]
         for c in cr:
             c.wait_recv()
-        got = dot(swap[...], zret[d].reshape(packed_rows, chunk)).astype(BF16)
-        ypack[d] = got.reshape(ypack.shape[1:])
-        cs = [send(ypack.at[d, ys[k]], yret.at[d, yl, h], y_peers[k - 1]) for k in (1, 2, 3)]
-        yret[d, yl, h] = ypack[d, y]
+        slots = zret[d].reshape(packed_rows, chunk)
+        for c in range(2):
+            got = dot(weighs[c][0], slots) + dot(weighs[c][1], slots)
+            ypack[d, :, :, c * chunk:(c + 1) * chunk] = got.astype(BF16).reshape(SIDE, tokens, chunk)
+        cs = [send(ypack.at[d, ys[k]], yret.at[d, h, :, d_half(yl)], y_peers[k - 1]) for k in (1, 2, 3)]
+        yret[d, h, :, d_half(yl)] = ypack[d, y]
         return cs
 
-    w_hi = table.astype(BF16)
-    w_lo = (table - w_hi.astype(F32)).astype(BF16)
-
     def combine(d, cr):
-        hi = [dot_t(w_hi, slot_of[d, c]).astype(BF16) for c in range(2)]
-        lo = [dot_t(w_lo, slot_of[d, c]).astype(BF16) for c in range(2)]
         for c in cr:
             c.wait_recv()
-        parts = []
-        for k in range(2):
-            slots = yret[d, k].reshape(packed_rows // 2, chunk)
-            for c in range(2):
-                parts.append(dot(hi[c], slots) + dot(lo[c], slots))
-        return jnp.concatenate(parts, axis=1)
-
-    r = gathered(C)
+        return yret[d, 0].astype(F32) + yret[d, 1].astype(F32)
+
+    gathered(C)
     f_d.wait()
-    c_d.wait_recv()
-    psend[C, :, 0:hid] = dot_t(r, wd[hidden(other), :]).astype(BF16)
-    cp[C] = send(psend.at[C, :, 0:hid], precv.at[C, :, 0:hid], mate)
-    d_part = dot_t(r, wd[hidden(yl), :])
-
-    c_act.wait_recv()
+    for c in c_d:
+        c.wait_recv()
+    psend_c[...] = in_blocks(dot_t(rbuf[C], wd[hidden(other), :])).astype(BF16)
+    cp[C] = pair(psend_c, precv_c)
+    cp[B] = pair(psend.at[B], precv.at[B])
+    d_part[...] = in_blocks(dot_t(rbuf[C], wd[hidden(yl), :]))
 
     def f_block(k):
-        at_k = pl.ds(pl.multiple_of(k * block, block), block)
-        a = jnp.concatenate([act[0, at_k, :], act[1, at_k, :]], axis=1)
+        a = jnp.concatenate([act[0, k], act[1, k]], axis=1)
         total = 0.0
         for c in range(2):
             total = total + dot(dot(pick_t[c], a).astype(BF16), wd[:, c * chunk:(c + 1) * chunk])
         return total
 
-    cr_f = reduce_start(0, f_block)
-
-    cp[B].wait_recv()
-    gu = part[B] + precv[B].astype(F32)
-    gate, up = gu[:, :hid], gu[:, hid:]
-    sigma = jax.nn.sigmoid(gate)
-    by_gate = up * sigma * (1.0 + gate * (1.0 - sigma))
-    by_up = gate * sigma
-    cp[C].wait_recv()
-    d_act = d_part + precv[C, :, 0:hid].astype(F32)
-    dgu[yl, :, 0:hid] = (d_act * by_gate).astype(BF16)
-    dgu[yl, :, hid:2 * hid] = (d_act * by_up).astype(BF16)
-    c_dgu = send(dgu.at[yl], dgu.at[yl], mate)
-
+    cr_f = reduce_start(0, f_block, c_act)
     cr_f = reduce_finish(0, cr_f)
 
+    c_dgu = []
+    for n, k in enumerate(order):
+        cp[C][n].wait_recv()
+        cp[B][n].wait_recv()
+        gu = part[B, k] + precv[B, k].astype(F32)
+        gate, up = gu[:, :hid], gu[:, hid:]
+        sigma = jax.nn.sigmoid(gate)
+        d_act = d_part[k] + precv_c[k].astype(F32)
+        dgu[yl, k, :, 0:hid] = (d_act * up * sigma * (1.0 + gate * (1.0 - sigma))).astype(BF16)
+        dgu[yl, k, :, hid:2 * hid] = (d_act * gate * sigma).astype(BF16)
+        c_dgu.append(send(dgu.at[yl, k], dgu.at[yl, k], mate))
+
     def b_block(k):
-        at_k = pl.ds(pl.multiple_of(k * block, block), block)
         total = 0.0
         for s in range(2):
             for c in range(2):
-                a = dot(pick_t[c], dgu[s, at_k, :]).astype(BF16)
+                a = dot(pick_t[c], dgu[s, k]).astype(BF16)
                 total = total + dot_t(a, w1[s, c * chunk:(c + 1) * chunk, :])
         return total
 
-    c_dgu.wait_recv()
-    cr_b = reduce_start(1, b_block)
+    cr_b = reduce_start(1, b_block, c_dgu)
     cr_f = z_return(0, cr_f)
     cr_b = reduce_finish(1, cr_b)
     cr_f = y_return(0, cr_f)
@@ -447,22 +459,25 @@
             V(args[8].shape, F32),
             V(args[9].shape, jnp.int32),
             V(args[10].shape, F32),
-            V(slots.shape, BF16),
+            V(slots.shape[1:], BF16),
             V((tokens, width), BF16),
             V((tokens, width), BF16),
             V((2, tokens, width), BF16),
-            V((3, 2, 2) + packed[1:], BF16),
-            V((3,) + packed, BF16),
+            V((SIDE, tokens, 128), F32),
+            V((3, SIDE, tokens, half_d), BF16),
             V((3,) + packed, BF16),
             V((3, SIDE) + packed, BF16),
             V((3, rows, half_d), BF16),
             V((2, half_d, 2 * hid), BF16),
             V((2 * hid, half_d), BF16),
-            V((2, rows, 2 * hid), F32),
-            V((3, rows, 2 * hid), BF16),
-            V((3, rows, 2 * hid), BF16),
-            V((2, rows, hid), BF16),
-            V((2, rows, 2 * hid), BF16),
+            V((2, SIDE, block, 2 * hid), F32),
+            V((SIDE, block, hid), F32),
+            V((2, SIDE, block, 2 * hid), BF16),
+            V((2, SIDE, block, 2 * hid), BF16),
+            V((SIDE, block, hid), BF16),
+            V((SIDE, block, hid), BF16),
+            V((2, SIDE, block, hid), BF16),
+            V((2, SIDE, block, 2 * hid), BF16),
             V((2, 3) + packed, F32),
             V((2,) + packed, BF16),
             V((2,) + packed, BF16),
@@ -470,11 +485,10 @@
             V((2, 2) + packed, BF16),
             V((2,) + packed, BF16),
             V((2,) + packed, BF16),
-            V((2,) + packed, BF16),
-            V((2, 2, 2) + packed[1:], BF16),
+            V((2, SIDE, tokens, half_d), BF16),
+            V((2, 2, tokens, width), BF16),
             V((2, block, 2 * block), BF16),
             V((2, 2 * block, block), BF16),
-            V((2 * block, 2 * block), BF16),
             pltpu.SemaphoreType.DMA((N_SEMS,)),
             pltpu.SemaphoreType.DMA((N_SEMS,)),
             pltpu.SemaphoreType.DMA((10,)),

time: 106 us -> 104 us (0.981)
  the two profiles are of different devices: /device:TPU:2 before, /device:TPU:32 now
where the time goes in v4:
time: 104 us
  Pallas kernels  101 us (97%)
  local copies, waits for them, and re-layouts  2.24 us (2%)
    pallas_call x1, Pallas kernels, local(): pl.pallas_call(kernel, out_shape=(out, out), in_specs=[hbm] * 12, out_spe...  101 us
    unnamed x4, local copies, waits for them, and re-layouts  2.24 us

profile of v4, /device:TPU:32, one launch (start us, length us, event | category | flops | bytes accessed | tf_op | source)
XLA Modules:
  0.0 104.0 jit_solution(5197788448374869006)
XLA Ops:
  0.6 101.2 %shard_map.131 = (bf16[1,16,3584]{2,1,0:T(8,128)(2,1)}, bf16[1,16,3584]{2,1,0:T(8,128)(2,1)}) custom-call(bf16[1,16,3584]{2,1,0:T(8,128)(2,1)} %acts.1, bf16[1,16,3584]{2,1,0:T(8,128)(2,1)} %grads.1, bf16[1,16,3584]{2,1,0:T(8,128)(2,1)} %saved_in.1, f32[1,3584]{1,0:T(1,128)} %gain_in.1, bf16[1,3584,128]{2,1,0:T(8,128)(2,1)} %gate_w.1, ...), custom_call_target="tpu_custom_call" | custom-call | tf_op jit(solution)/shard_map/pallas_call | solution.py:450
  101.8 0.0 copy-start
  101.8 1.6 %copy.16 = bf16[1,16,3584]{2,1,0:T(8,128)(2,1)} copy(bf16[1,16,3584]{2,1,0:T(8,128)(2,1)} %get-tuple-element.4) | data formatting | bytes 229376
  103.4 0.0 copy-done
  103.4 0.6 copy.17
Async XLA Ops:
  101.8 1.6 %copy-start = (bf16[1,16,3584]{2,1,0:T(8,128)(2,1)S(1)}, bf16[1,16,3584]{2,1,0:T(8,128)(2,1)}, u32[]{:S(2)}) copy-start(bf16[1,16,3584]{2,1,0:T(8,128)(2,1)} %get-tuple-element.5) | copy-start | bytes 344068

commit v5 on v4

--- a/solution.py
+++ b/solution.py
@@ -49,11 +49,11 @@
 
 def kernel(
     acts, grads, saved_in, gain_in, gate_w, up_w, down_w, fr_in, fg_in, br_in, bg_in, slot_in,
-    out_ref, din_ref,
+    out_ref,
     saved_ref, gain_ref, f_routes, f_gates, b_routes, b_gates, slot_of,
     in_buf, cot_buf, norm_buf, tab, ytok, zsend, xbuf, rbuf, w1, wd, part, d_part, psend, precv,
     psend_c, precv_c, act, dgu, mine, rsopp, rsrecv, rssend, rsin, zpack, zret, ypack, yret,
-    pick, pick_t,
+    pick, pick_t, row_mask, token_mask,
     send_sem, recv_sem, copy_sem,
 ):
     tokens, width = saved_ref.shape[1], saved_ref.shape[2]
@@ -223,7 +223,14 @@
             fetch(up_w.at[0, d_half(yl), :], w1.at[yl, :, hid:2 * hid])]
     f_d = fetch(down_w.at[0, :, d_half(yl)], wd.at[hidden(yl), :])
 
+    def matches(shape, dim, c):
+        row = lax.broadcasted_iota(jnp.int32, shape, dim)
+        token = lax.broadcasted_iota(jnp.int32, shape, 1 - dim)
+        return ((sixth(row) >> 2) & 1 == c) & (sixth(row) & 3 == token // tokens)
+
     for c in range(2):
+        row_mask[c] = jnp.where(matches(row_mask.shape[1:], 0, c), 1.0, 0.0).astype(BF16)
+        token_mask[c] = jnp.where(matches(token_mask.shape[1:], 1, c), 1.0, 0.0).astype(BF16)
         pick[c] = one_hot(pick.shape[1:], lambda i, j: j == unpacked(i, c))
         pick_t[c] = one_hot(pick_t.shape[1:], lambda i, j: i == unpacked(j, c))
 
@@ -234,14 +241,8 @@
     w_hi = table.astype(BF16)
     w_lo = (table - w_hi.astype(F32)).astype(BF16)
 
-    def matches(shape, dim, c):
-        row = lax.broadcasted_iota(jnp.int32, shape, dim)
-        token = lax.broadcasted_iota(jnp.int32, shape, 1 - dim)
-        return ((sixth(row) >> 2) & 1 == c) & (sixth(row) & 3 == token // tokens)
-
-    to_rows, to_tokens = (packed_rows, SIDE * tokens), (SIDE * tokens, packed_rows)
     selects = [
-        [jnp.where(matches(to_rows, 0, c), dot_t(slot_of[d], chosen), 0.0).astype(BF16) for c in range(2)]
+        [dot_t(slot_of[d], chosen).astype(BF16) * row_mask[c] for c in range(2)]
         for d in range(2)
     ]
 
@@ -357,7 +358,7 @@
 
     def y_return(d, cr):
         weighs = [
-            [jnp.where(matches(to_tokens, 1, c), dot_t(w, slot_of[d]), 0.0).astype(BF16) for w in (w_hi, w_lo)]
+            [dot_t(w, slot_of[d]).astype(BF16) * token_mask[c] for w in (w_hi, w_lo)]
             for c in range(2)
         ]
         for c in cr:
@@ -427,7 +428,7 @@
     scale = scale_of(v)
     dn = combine(1, cr_b) * gain
     d_in = scale * dn - v * (scale * scale * scale) * jnp.mean(dn * v, axis=-1, keepdims=True)
-    din_ref[0] = (cot_buf[...].astype(F32) + d_in).astype(BF16)
+    out_ref[1] = (cot_buf[...].astype(F32) + d_in).astype(BF16)
 
     for c in started:
         c.wait_send()
@@ -443,15 +444,15 @@
     half_d, chunk = width // 2, width // 4
     args = args[:7] + tuple(jnp.swapaxes(a, 1, 2) for a in args[7:])
     vmem, hbm = pl.BlockSpec(memory_space=pltpu.VMEM), pl.BlockSpec(memory_space=pl.ANY)
-    out = jax.ShapeDtypeStruct((1, tokens, width), BF16)
+    out = jax.ShapeDtypeStruct((2, tokens, width), BF16)
     slots = constants()
     V = pltpu.VMEM
     packed = (SIDE, 2 * per, chunk)
-    return pl.pallas_call(
+    both = pl.pallas_call(
         kernel,
-        out_shape=(out, out),
+        out_shape=out,
         in_specs=[hbm] * 12,
-        out_specs=(vmem, vmem),
+        out_specs=vmem,
         scratch_shapes=[
             V(args[2].shape, BF16),
             V(args[3].shape, F32),
@@ -489,6 +490,8 @@
             V((2, 2, tokens, width), BF16),
             V((2, block, 2 * block), BF16),
             V((2, 2 * block, block), BF16),
+            V((2, 2 * block, SIDE * tokens), BF16),
+            V((2, SIDE * tokens, 2 * block), BF16),
             pltpu.SemaphoreType.DMA((N_SEMS,)),
             pltpu.SemaphoreType.DMA((N_SEMS,)),
             pltpu.SemaphoreType.DMA((10,)),
@@ -497,6 +500,7 @@
             collective_id=0, has_side_effects=True, vmem_limit_bytes=58 * 1024 * 1024
         ),
     )(*args, slots)
+    return both[0:1], both[1:2]
 
 
 def solution(mesh):

time: 104 us -> 104 us (level)
  the two profiles are of different devices: /device:TPU:32 before, /device:TPU:2 now
where the time goes in v5:
time: 104 us; the launch traced here: 103 us
  Pallas kernels  101 us (97%)
  local copies, waits for them, and re-layouts  1.65 us (2%)
    pallas_call x1, Pallas kernels, local(): pl.pallas_call(kernel, out_shape=out, in_specs=[hbm] * 12, out_specs=vmem...  101 us

profile of v5, /device:TPU:2, one launch (start us, length us, event | category | flops | bytes accessed | tf_op | source)
XLA Modules:
  0.0 103.4 jit_solution(7707006616969249275)
XLA Ops:
  0.6 101.1 %shard_map.131 = bf16[2,16,3584]{2,1,0:T(8,128)(2,1)} custom-call(bf16[1,16,3584]{2,1,0:T(8,128)(2,1)} %acts.1, bf16[1,16,3584]{2,1,0:T(8,128)(2,1)} %grads.1, bf16[1,16,3584]{2,1,0:T(8,128)(2,1)} %saved_in.1, f32[1,3584]{1,0:T(1,128)} %gain_in.1, bf16[1,3584,128]{2,1,0:T(8,128)(2,1)} %gate_w.1, bf16[1,3584,128]{2,1,0:T(8,128)(2,1)} %up_w.1, ...), custom_call_target="tpu_custom_call" | custom-call | tf_op jit(solution)/shard_map/pallas_call | solution.py:451
  101.7 1.7 %fusion = (bf16[1,16,3584]{2,1,0:T(8,128)(2,1)}, bf16[1,16,3584]{2,1,0:T(8,128)(2,1)}) fusion(bf16[2,16,3584]{2,1,0:T(8,128)(2,1)} %shard_map.131), kind=kLoop, calls=%fused_computation | loop fusion | bytes 458752 | tf_op jit(solution)/shard_map/slice | solution.py:503
